TPU v7x, 256 devices: a whole 4x4x8 slice. The times are simulated.
256 devices in a mesh: dp: 16 (over y, x_lo, core), sp: 16 (over z, x_hi).
Axes of the slice: x: 4 (x_hi: 2, x_lo: 2; x = x_hi * 2 + x_lo), y: 4, z: 8, core: 2. Of those that a mesh axis runs over, the one named last changes fastest.
Arguments:
- query: bfloat16 [16, 2048, 2048], P('dp', 'sp'), may hold values from -6 to 6
- key_in: bfloat16 [16, 2048, 2048], P('dp', 'sp'), may hold values from -6 to 6
- value: bfloat16 [16, 2048, 2048], P('dp', 'sp'), may hold values from -6 to 6
- bucket: int32 [16], P('dp'), may hold values from 0 to 1, as said below
- clip_cost: int32 [16, 4], P('dp'), may hold values from 0 to 999
- positions: int32 [3, 16, 2048], P(None, 'dp', 'sp'), may hold values from 0 to 63
- out_weight: bfloat16 [2048, 3072], P('sp'), may hold values from -0.125 to 0.125
- cotangent: bfloat16 [16, 2048, 3072], P('dp', 'sp'), may hold values from -6 to 6
Outputs:
- mixed: bfloat16 [16, 2048, 3072], P('dp', 'sp')
- grad_query: bfloat16 [16, 2048, 2048], P('dp', 'sp')
- grad_key: bfloat16 [16, 2048, 2048], P('dp', 'sp')
- grad_value: bfloat16 [16, 2048, 2048], P('dp', 'sp')
- grad_weight: float32 [2048, 3072], P('sp', 'dp')
Inputs may be any that keep to these rules, and one draw needn't show every extreme that they name: Exactly half of the rows have bucket 1.
All inputs are finite; a program needn't handle non-finite values.
Results may differ from a plain program's by a relative error of at most 0.023.
Values may be sent and summed in bfloat16 or wider, within the bound.
A program may use at most 128 MiB of HBM per device.

v0:
```python
import jax
import jax.numpy as jnp
import numpy as np
from jax import lax
from jax.sharding import PartitionSpec as P

HD = 128
CLIPS = 4


def for_sending(array):

    def short(part):
        return part.astype(jnp.bfloat16) if part.dtype == jnp.float32 else part

    return jax.tree.map(short, array)


def rotary_layout(head_dim):
    quarter = head_dim // 4
    rest_span = (head_dim - quarter) // 2
    part_spans = (quarter, rest_span, head_dim - quarter - rest_span)
    partner = []
    signs = []
    axis_of = []
    frequency = []
    offset = 0
    for part_index in range(3):
        part_span = part_spans[part_index]
        half_span = part_span // 2
        for inner_dim in range(part_span):
            pair_index = inner_dim % half_span
            if inner_dim < half_span:
                partner.append(offset + inner_dim + half_span)
                signs.append(-1.0)
            else:
                partner.append(offset + inner_dim - half_span)
                signs.append(1.0)
            axis_of.append(part_index)
            frequency.append(10000.0 ** (-pair_index / half_span))
        offset += part_span
    return (np.array(partner), np.array(signs), np.array(axis_of), np.array(frequency))


def rotary_tables(places, head_dim):
    partner, signs, axis_of, frequency = rotary_layout(head_dim)
    angles = (
        jnp.transpose(places.astype(jnp.float32)[axis_of])
        * jnp.asarray(frequency, jnp.float32)[None, :]
    )
    return (jnp.cos(angles), jnp.sin(angles) * jnp.asarray(signs, jnp.float32)[None, :])


def spin(flat, cosine, sine_signed, direction, head_dim):
    partner = rotary_layout(head_dim)[0]
    count = flat.shape[0]
    values = flat.astype(jnp.float32).reshape(count, -1, head_dim)
    turned = (
        values * cosine[:, None, :] + direction * values[..., partner] * sine_signed[:, None, :]
    )
    return turned.reshape(count, -1)


def deal_tables(costs, wide):
    slots = jnp.arange(costs.shape[0], dtype=jnp.int32)
    above = (costs[None, :] > costs[:, None]) | (costs[None, :] == costs[:, None]) & (
        slots[None, :] < slots[:, None]
    )
    rank = jnp.sum(above.astype(jnp.int32), axis=1)
    order = jnp.sum(jnp.where(rank[None, :] == slots[:, None], slots[None, :], 0), axis=1)
    rank = jnp.where(wide == 1, slots, rank)
    order = jnp.where(wide == 1, slots, order)
    return (rank, order)


def take_blocks(rows, index):
    count = rows.shape[0]
    blocks = rows.reshape(index.shape[0], count // index.shape[0], -1)
    return jnp.take(blocks, index, axis=0).reshape(count, -1)


def contract_last(left, right):
    return lax.dot_general(
        left, right, (((1,), (1,)), ((), ())), preferred_element_type=jnp.float32
    )


def contract_first(left, right):
    return lax.dot_general(
        left, right, (((0,), (0,)), ((), ())), preferred_element_type=jnp.float32
    )


def block_probs(rows_query, rows_clip, key_h, clip_ids):
    scores = contract_last(rows_query, key_h) * HD ** (-0.5)
    return jnp.where(rows_clip[:, None] == clip_ids[None, :], scores, -1e30)


def attend_forward(query_h, key_h, value_h, clip_ids, block_rows):
    count = query_h.shape[0]
    blocks = count // block_rows

    def one_block(pieces):
        rows_query, rows_clip = pieces
        scores = block_probs(rows_query, rows_clip, key_h, clip_ids)
        top = jnp.max(scores, axis=1, keepdims=True)
        raw_weights = jnp.exp(scores - top)
        total = jnp.sum(raw_weights, axis=1, keepdims=True)
        probs_low = (raw_weights / total).astype(jnp.bfloat16)
        attended = jnp.dot(probs_low, value_h, preferred_element_type=jnp.float32).astype(
            jnp.bfloat16
        )
        return (attended, top, total)

    attended, top, total = lax.map(
        one_block, (query_h.reshape(blocks, block_rows, -1), clip_ids.reshape(blocks, block_rows))
    )
    return (attended.reshape(count, -1), top, total)


def attend_backward(query_h, key_h, value_h, grad_h, clip_ids, top, total, block_rows):
    count = query_h.shape[0]
    blocks = count // block_rows
    factor = HD ** (-0.5)

    def one_block(carry, pieces):
        grad_key, grad_value = carry
        rows_query, rows_clip, rows_grad, rows_top, rows_total = pieces
        scores = block_probs(rows_query, rows_clip, key_h, clip_ids)
        probs = jnp.exp(scores - rows_top) / rows_total
        probs_low = probs.astype(jnp.bfloat16)
        grad_probs = contract_last(rows_grad, value_h)
        centre = jnp.sum(probs * grad_probs, axis=1, keepdims=True)
        grad_scores = (probs * (grad_probs - centre) * factor).astype(jnp.bfloat16)
        grad_query = jnp.dot(grad_scores, key_h, preferred_element_type=jnp.float32).astype(
            jnp.bfloat16
        )
        grad_key = grad_key + contract_first(grad_scores, rows_query)
        grad_value = grad_value + contract_first(probs_low, rows_grad)
        return ((grad_key, grad_value), grad_query)

    empty = jnp.zeros((count, query_h.shape[1]), jnp.float32)
    pieces = (
        query_h.reshape(blocks, block_rows, -1),
        clip_ids.reshape(blocks, block_rows),
        grad_h.reshape(blocks, block_rows, -1),
        top,
        total,
    )
    (grad_key, grad_value), grad_query = lax.scan(one_block, (empty, empty), pieces)
    return (
        grad_query.reshape(count, -1),
        grad_key.astype(jnp.bfloat16),
        grad_value.astype(jnp.bfloat16),
    )


def local(query, key_in, value, bucket, clip_cost, positions, out_weight, cotangent):
    local_rows = query.shape[1]
    model_width = cotangent.shape[2]
    cosine, sine_signed = rotary_tables(positions[:, 0, :], HD)
    rot_query = spin(query[0], cosine, sine_signed, 1.0, HD).astype(jnp.bfloat16)[None]
    rot_key = spin(key_in[0], cosine, sine_signed, 1.0, HD).astype(jnp.bfloat16)[None]
    head_query, head_key, head_value = (
        lax.all_to_all(rot_query, "sp", split_axis=2, concat_axis=1, tiled=True),
        lax.all_to_all(rot_key, "sp", split_axis=2, concat_axis=1, tiled=True),
        lax.all_to_all(value, "sp", split_axis=2, concat_axis=1, tiled=True),
    )
    group_rows = head_query.shape[1]
    wide = bucket[0]
    rank, order = deal_tables(clip_cost[0], wide)
    clip_ids = jnp.where(
        wide == 1,
        jnp.zeros((group_rows,), jnp.int32),
        jnp.arange(group_rows, dtype=jnp.int32) // (group_rows // CLIPS),
    )
    local_heads = head_query.shape[2] // HD
    block_rows = min(512, group_rows)
    attended_parts = []
    saved_stats = []
    for head in range(local_heads):
        lower = head * HD
        attended_h, top, total = attend_forward(
            head_query[0, :, lower : lower + HD],
            head_key[0, :, lower : lower + HD],
            head_value[0, :, lower : lower + HD],
            clip_ids,
            block_rows,
        )
        attended_parts.append(attended_h)
        saved_stats.append((top, total))
    attended = take_blocks(jnp.concatenate(attended_parts, axis=1), order)
    attended_tokens = lax.all_to_all(
        for_sending(attended[None]), "sp", split_axis=1, concat_axis=2, tiled=True
    )[0]
    piece = lax.all_gather(out_weight, "sp", axis=0, tiled=True)
    columns = lax.slice_in_dim(attended_tokens, 0, piece.shape[0], axis=1)
    projected = jnp.zeros((local_rows, model_width), jnp.float32) + jnp.dot(
        columns, piece, preferred_element_type=jnp.float32
    )
    mixed = projected.astype(jnp.bfloat16)[None]
    start = jnp.int32(0)
    grad_attended = jnp.zeros((group_rows, attended.shape[1]), jnp.float32)
    grad_weight = jnp.zeros((attended.shape[1], model_width), jnp.float32)
    rows = lax.all_gather(cotangent, "sp", axis=1, tiled=True)[0]
    grad_rows = contract_last(rows, out_weight)
    grad_attended = lax.dynamic_update_slice_in_dim(grad_attended, grad_rows, start, 0)
    seen = lax.dynamic_slice_in_dim(attended, start, rows.shape[0], 0)
    grad_weight = grad_weight + contract_first(seen, rows)
    grad_attended, grad_weight = (grad_attended, grad_weight)
    grad_attended = take_blocks(grad_attended.astype(jnp.bfloat16), rank)
    query_parts = []
    key_parts = []
    value_parts = []
    for head in range(local_heads):
        lower = head * HD
        top, total = saved_stats[head]
        grad_q, grad_k, grad_v = attend_backward(
            head_query[0, :, lower : lower + HD],
            head_key[0, :, lower : lower + HD],
            head_value[0, :, lower : lower + HD],
            grad_attended[:, lower : lower + HD],
            clip_ids,
            top,
            total,
            block_rows,
        )
        query_parts.append(grad_q)
        key_parts.append(grad_k)
        value_parts.append(grad_v)
    returned = (
        lax.all_to_all(
            for_sending(jnp.concatenate(query_parts, axis=1)[None]),
            "sp",
            split_axis=1,
            concat_axis=2,
            tiled=True,
        ),
        lax.all_to_all(
            for_sending(jnp.concatenate(key_parts, axis=1)[None]),
            "sp",
            split_axis=1,
            concat_axis=2,
            tiled=True,
        ),
        lax.all_to_all(
            for_sending(jnp.concatenate(value_parts, axis=1)[None]),
            "sp",
            split_axis=1,
            concat_axis=2,
            tiled=True,
        ),
    )
    grad_query = spin(returned[0][0], cosine, sine_signed, -1.0, HD).astype(jnp.bfloat16)[None]
    grad_key = spin(returned[1][0], cosine, sine_signed, -1.0, HD).astype(jnp.bfloat16)[None]
    summed = lax.psum(grad_weight.astype(jnp.bfloat16), "dp").astype(jnp.float32)
    share_cols = model_width // lax.axis_size("dp")
    weight_share = lax.dynamic_slice_in_dim(
        summed, lax.axis_index("dp") * share_cols, share_cols, 1
    )
    return (mixed, grad_query, grad_key, returned[2], weight_share)


def solution(mesh):
    in_specs = (
        P("dp", "sp", None),
        P("dp", "sp", None),
        P("dp", "sp", None),
        P("dp"),
        P("dp", None),
        P(None, "dp", "sp"),
        P("sp", None),
        P("dp", "sp", None),
    )
    out_specs = (
        P("dp", "sp", None),
        P("dp", "sp", None),
        P("dp", "sp", None),
        P("dp", "sp", None),
        P("sp", "dp"),
    )
    return jax.shard_map(local, mesh=mesh, in_specs=in_specs, out_specs=out_specs, check_vma=False)
```

profile of v0, /device:TPU:1, one launch (start us, length us, event | category | flops | bytes accessed | tf_op | source)
XLA Modules:
  0.0 573.7 jit_solution(7741272751904696203)
XLA Ops:
  11.3 1.7 gather_fusion.1
  13.0 1.7 gather_fusion.2
  15.7 1.8 bitcast_multiply_fusion.6
  18.5 8.7 %copy.217 = bf16[1,128,2048]{1,0,2:T(2,128)(2,1)S(1)} copy(bf16[1,128,2048]{1,2,0:T(8,128)(2,1)S(1)} %get-tuple-element.279) | data formatting | bytes 1048576 | tf_op jit(solution)/shard_map/convert_element_type | solution.py:162
  27.7 11.5 %reduce = bf16[2048,128]{1,0:T(8,128)(2,1)S(1)} reduce(bf16[2048,1,128]{2,1,0:T(2,128)(2,1)S(1)} %bitcast.228, bf16[]{:T(256)} %broadcast.165), dimensions={1}, to_apply=%bitcast.171.reduce_sub_computation | reduce | bytes 1048578
  40.2 11.8 %all-to-all-start = ((bf16[16,2,8192]{2,1,0:T(2,128)(2,1)}), bf16[16,2,8192]{2,1,0:T(2,128)(2,1)S(1)}, u32[]{:S(2)}, u32[]{:S(2)}) async-start(bf16[16,2,8192]{2,1,0:T(2,128)(2,1)} %reshape.306), calls=%async_computation | async-start | bytes 1048576 | tf_op jit(solution)/shard_map/all_to_all | solution.py:165
  51.9 8.1 %copy.216 = bf16[1,128,2048]{1,0,2:T(2,128)(2,1)S(1)} copy(bf16[1,128,2048]{1,2,0:T(8,128)(2,1)S(1)} %get-tuple-element.278) | data formatting | bytes 1048576 | tf_op jit(solution)/shard_map/convert_element_type | solution.py:163
  60.1 11.5 %reduce.1 = bf16[2048,128]{1,0:T(8,128)(2,1)S(1)} reduce(bf16[2048,1,128]{2,1,0:T(2,128)(2,1)S(1)} %bitcast.230, bf16[]{:T(256)} %broadcast.165), dimensions={1}, to_apply=%bitcast.170.reduce_sub_computation | reduce | bytes 1048578
  72.5 3.3 all-to-all-done
  75.8 5.8 %all-to-all-start.1 = ((bf16[16,2,8192]{2,1,0:T(2,128)(2,1)}), bf16[16,2,8192]{2,1,0:T(2,128)(2,1)S(1)}, u32[]{:S(2)}, u32[]{:S(2)}) async-start(bf16[16,2,8192]{2,1,0:T(2,128)(2,1)} %reshape.308), calls=%async_computation.1 | async-start | bytes 1048576 | tf_op jit(solution)/shard_map/all_to_all | solution.py:166
  83.4 11.5 %reduce.2 = bf16[2048,128]{1,0:T(8,128)(2,1)S(1)} reduce(bf16[2048,1,128]{2,1,0:T(2,128)(2,1)S(1)} %bitcast.233, bf16[]{:T(256)} %broadcast.165), dimensions={1}, to_apply=%bitcast.135.reduce_sub_computation | reduce | bytes 1048578
  96.5 3.9 all-to-all-done.1
  100.4 5.3 all-to-all-start.2
  107.0 2.2 reshape.309
  110.3 12.6 %all-to-all-done.2 = bf16[16,2,8192]{2,1,0:T(2,128)(2,1)} async-done(((bf16[16,2,8192]{2,1,0:T(2,128)(2,1)}), bf16[16,2,8192]{2,1,0:T(2,128)(2,1)}, u32[]{:S(2)}, u32[]{:S(2)}) %all-to-all-start.2) | async-done | bytes 524320 | tf_op jit(solution)/shard_map/all_to_all | solution.py:167
  122.9 2.2 reshape.311
  125.5 14.6 %while.30 = (s32[]{:T(128)}, bf16[4,512,128]{2,1,0:T(8,128)(2,1)S(1)}, f32[4,512,1]{1,2,0:T(1,128)S(1)}, f32[4,512,1]{1,2,0:T(1,128)S(1)}, s32[4,512]{1,0:T(4,12...) while((s32[]{:T(128)}, ...), condition=%wide.region_3.4_spmd.clone, body=%wide.region_0.3_spmd.clone.sunk | while | flops 546391040 | bytes 13934710 | solution.py:115
  125.6 1.9 fusion.95
  129.2 1.9 fusion.95
  132.9 1.9 fusion.95
  136.5 1.9 fusion.95
  141.7 8.1 %copy.215 = bf16[1,2048,128]{2,0,1:T(2,128)(2,1)S(1)} copy(bf16[1,2048,128]{2,1,0:T(8,128)(2,1)S(1)} %bitcast.219) | data formatting | bytes 1048576 | tf_op jit(solution)/shard_map/broadcast_in_dim;reshape | solution.py:194
  149.8 12.7 %reduce.3 = bf16[2048,128]{1,0:T(8,128)(2,1)} reduce(bf16[2048,1,128]{2,1,0:T(2,128)(2,1)S(1)} %bitcast.234, bf16[]{:T(256)} %broadcast.165), dimensions={1}, to_apply=%bitcast.169.reduce_sub_computation | reduce | bytes 1048578
  162.5 2.0 reshape.312
  164.5 4.4 all-to-all-start.3
  168.9 56.1 %all-gather.5.cloned.1.call-done = bf16[1,2048,3072]{2,1,0:T(8,128)(2,1)} async-done(((bf16[1,128,3072]{2,1,0:T(8,128)(2,1)}), bf16[1,2048,3072]{2,1,0:T(8,128)(2,1)}) %all-gather.5.cloned.1.call-update) | async-done | bytes 12582928 | tf_op jit(solution)/shard_map/all_gather | solution.py:205
  225.0 8.1 %fusion.44 = bf16[2048,128]{1,0:T(8,128)(2,1)S(1)} fusion(bf16[128,3072]{1,0:T(8,128)(2,1)} %param.32, bf16[1,2048,3072]{2,1,0:T(8,128)(2,1)} %all-gather.5.cloned.1.call-done), kind=kOutput, calls=%fused_computation.75 | convolution fusion | flops 1610874880 | bytes 13893632 | tf_op jit(solution)/shard_map/dot_general | solution.py:83
  234.8 53.8 %while.31 = (s32[]{:T(128)}, f32[2048,128]{1,0:T(8,128)S(1)}, f32[2048,128]{1,0:T(8,128)}, bf16[4,512,128]{2,1,0:T(8,128)(2,1)}, s32[4,512]{1,0:T(4,128)S(1)}, /...) while((s32[]{:T(128)}, f32[2048,128]{1,0:T(8,128)S(1)}, ...), condition=%wide.region_8.10_spmd.clone, body=%wide.region_6.9_spmd.clone.sunk | while | flops 1355892224 | bytes 86155168 | solution.py:150
  237.9 2.0 copy-done
  240.4 2.1 convolution_add_fusion.4
  242.6 2.4 fusion.109
  245.0 2.8 convolution_add_fusion.5
  249.3 1.7 multiply_reduce_fusion.2
  251.0 2.0 copy-done
  253.6 2.1 convolution_add_fusion.4
  255.7 2.4 fusion.109
  258.1 3.2 convolution_add_fusion.5
  262.8 1.7 multiply_reduce_fusion.2
  264.5 2.0 copy-done
  267.1 2.1 convolution_add_fusion.4
  269.2 2.4 fusion.109
  271.6 3.2 convolution_add_fusion.5
  278.0 2.0 copy-done
  280.6 2.1 convolution_add_fusion.4
  282.7 2.4 fusion.109
  285.1 3.5 convolution_add_fusion.5
  288.6 2.2 convert_bitcast_fusion
  290.8 8.3 %copy.213 = bf16[1,2048,128]{2,0,1:T(2,128)(2,1)S(1)} copy(bf16[1,2048,128]{2,1,0:T(8,128)(2,1)S(1)} %get-tuple-element.283) | data formatting | bytes 1048576 | tf_op jit(solution)/shard_map/broadcast_in_dim | solution.py:240
  299.2 11.6 %reduce.4 = bf16[2048,128]{1,0:T(8,128)(2,1)S(1)} reduce(bf16[2048,1,128]{2,1,0:T(2,128)(2,1)S(1)} %bitcast.231, bf16[]{:T(256)} %broadcast.165), dimensions={1}, to_apply=%bitcast.167.reduce_sub_computation | reduce | bytes 1048578
  311.7 4.5 all-to-all-start.5
  316.2 8.1 %copy.214 = bf16[1,2048,128]{2,0,1:T(2,128)(2,1)S(1)} copy(bf16[1,2048,128]{2,1,0:T(8,128)(2,1)S(1)} %bitcast.239) | data formatting | bytes 1048576 | tf_op jit(solution)/shard_map/broadcast_in_dim;reshape | solution.py:233
  324.4 11.5 %reduce.5 = bf16[2048,128]{1,0:T(8,128)(2,1)S(1)} reduce(bf16[2048,1,128]{2,1,0:T(2,128)(2,1)S(1)} %bitcast.232, bf16[]{:T(256)} %broadcast.165), dimensions={1}, to_apply=%bitcast.168.reduce_sub_computation | reduce | bytes 1048578
  336.8 9.2 %all-to-all-start.4 = ((bf16[16,2,8192]{2,1,0:T(2,128)(2,1)}), bf16[16,2,8192]{2,1,0:T(2,128)(2,1)S(1)}, u32[]{:S(2)}, u32[]{:S(2)}) async-start(bf16[16,2,8192]{2,1,0:T(2,128)(2,1)} %reshape.314), calls=%async_computation.4 | async-start | bytes 1048576 | tf_op jit(solution)/shard_map/all_to_all | solution.py:232
  346.0 9.1 %fusion.40 = bf16[128,3072]{0,1:T(8,128)(2,1)} fusion(bf16[2048,128]{1,0:T(8,128)(2,1)S(1)} %bitcast.220, bf16[1,2048,3072]{2,1,0:T(8,128)(2,1)} %all-gather.5.cloned.1.call-done), kind=kOutput, calls=%fused_computation.68 | convolution fusion | flops 1611005952 | bytes 13893632 | tf_op jit(solution)/shard_map/dot_general | solution.py:89
  355.4 2.2 reshape.313
  358.0 1.8 copy.212
  359.8 11.5 %reduce.6 = bf16[2048,128]{1,0:T(8,128)(2,1)S(1)} reduce(bf16[2048,1,128]{2,1,0:T(2,128)(2,1)S(1)} %bitcast.229, bf16[]{:T(256)} %broadcast.165), dimensions={1}, to_apply=%bitcast.166.reduce_sub_computation | reduce | bytes 1048578
  372.2 9.3 %all-to-all-start.6 = ((bf16[16,2,8192]{2,1,0:T(2,128)(2,1)}), bf16[16,2,8192]{2,1,0:T(2,128)(2,1)}, u32[]{:S(2)}, u32[]{:S(2)}) async-start(bf16[16,2,8192]{2,1,0:T(2,128)(2,1)} %reshape.318), calls=%async_computation.6 | async-start | bytes 1048576 | tf_op jit(solution)/shard_map/all_to_all | solution.py:246
  381.6 43.7 %all-gather.3.cloned.1.call-done = bf16[2048,3072]{1,0:T(8,128)(2,1)} async-done(((bf16[128,3072]{1,0:T(8,128)(2,1)}), bf16[2048,3072]{1,0:T(8,128)(2,1)}) %all-gather.3.cloned.1.call-update) | async-done | bytes 12582928 | tf_op jit(solution)/shard_map/all_gather | solution.py:196
  425.2 7.3 %fusion.43 = bf16[1,128,3072]{2,1,0:T(8,128)(2,1)} fusion(bf16[128,2048]{0,1:T(8,128)(2,1)S(1)} %bitcast.235, bf16[2048,3072]{1,0:T(8,128)(2,1)} %all-gather.3.cloned.1.call-done), kind=kOutput, calls=%fused_computation.70 | convolution fusion | flops 1611005952 | bytes 13893632 | tf_op jit(solution)/shard_map/dot_general | solution.py:198
  432.5 116.2 %all-reduce.2.cloned.1.call-done = bf16[128,3072]{0,1:T(8,128)(2,1)} async-done(((bf16[128,3072]{0,1:T(8,128)(2,1)}), bf16[128,3072]{0,1:T(8,128)(2,1)}) %all-reduce.2.cloned.1.call-update) | async-done | bytes 786448 | tf_op jit(solution)/shard_map/psum | solution.py:256
  552.0 2.2 reshape.315
  556.6 1.7 gather_fusion.3
  563.4 2.2 reshape.319
  (209 shorter events, 50.2 us)
Async XLA Ops:
  7.2 4.1 copy-start.18
  7.2 217.8 %all-gather.5.cloned.1.call-start = ((), (), s32[]{:S(2)}) async-start(), calls=%async_computation.8 | async-start | bytes 13369344 | tf_op jit(solution)/shard_map/all_gather | solution.py:205
  9.2 5.5 copy-start.19
  9.2 5.5 copy-start.17
  9.3 6.1 %copy-start.15 = (f32[128]{0:T(128)S(1)}, f32[128]{0:T(128)}, u32[]{:S(2)}) copy-start(f32[128]{0:T(128)} %constant.113.clone) | copy-start | bytes 1540
  9.3 6.1 %copy-start.16 = (f32[128]{0:T(128)S(1)}, f32[128]{0:T(128)}, u32[]{:S(2)}) copy-start(f32[128]{0:T(128)} %constant.114.clone) | copy-start | bytes 1540
  39.2 43.2 %copy-start.13 = (bf16[1,128,2048]{2,1,0:T(8,128)(2,1)S(1)}, bf16[1,128,2048]{2,1,0:T(8,128)(2,1)}, u32[]{:S(2)}) copy-start(bf16[1,128,2048]{2,1,0:T(8,128)(2,1)} %param.28) | copy-start | bytes 1572868
  40.2 35.7 %all-to-all-start = ((bf16[16,2,8192]{2,1,0:T(2,128)(2,1)}), bf16[16,2,8192]{2,1,0:T(2,128)(2,1)S(1)}, u32[]{:S(2)}, u32[]{:S(2)}) async-start(bf16[16,2,8192]{2,1,0:T(2,128)(2,1)} %reshape.306), calls=%async_computation | async-start | bytes 1048576 | tf_op jit(solution)/shard_map/all_to_all | solution.py:165
  71.6 34.1 %copy-start.20 = (s32[1,4]{1,0:T(1,128)S(1)}, s32[1,4]{1,0:T(1,128)}, u32[]{:S(2)}) copy-start(s32[1,4]{1,0:T(1,128)} %param.30) | copy-start | bytes 52
  75.8 24.6 %all-to-all-start.1 = ((bf16[16,2,8192]{2,1,0:T(2,128)(2,1)}), bf16[16,2,8192]{2,1,0:T(2,128)(2,1)S(1)}, u32[]{:S(2)}, u32[]{:S(2)}) async-start(bf16[16,2,8192]{2,1,0:T(2,128)(2,1)} %reshape.308), calls=%async_computation.1 | async-start | bytes 1048576 | tf_op jit(solution)/shard_map/all_to_all | solution.py:166
  81.7 343.6 %all-gather.3.cloned.1.call-start = ((), (), s32[]{:S(2)}) async-start(), calls=%async_computation.7 | async-start | bytes 13369344 | tf_op jit(solution)/shard_map/all_gather | solution.py:196
  100.4 5.7 copy-start.11
  100.4 22.5 %all-to-all-start.2 = ((bf16[16,2,8192]{2,1,0:T(2,128)(2,1)}), bf16[16,2,8192]{2,1,0:T(2,128)(2,1)}, u32[]{:S(2)}, u32[]{:S(2)}) async-start(bf16[16,2,8192]{2,1,0:T(2,128)(2,1)} %reshape.310), calls=%async_computation.2 | async-start | bytes 1048576 | tf_op jit(solution)/shard_map/all_to_all | solution.py:167
  140.9 0.8 copy-start.6
  164.5 147.2 %all-to-all-start.3 = ((bf16[16,2,8192]{2,1,0:T(2,128)(2,1)}), bf16[16,2,8192]{2,1,0:T(2,128)(2,1)}, u32[]{:S(2)}, u32[]{:S(2)}) async-start(bf16[16,2,8192]{2,1,0:T(2,128)(2,1)} %reshape.312), calls=%async_computation.3 | async-start | bytes 1048576 | tf_op jit(solution)/shard_map/all_to_all | solution.py:193
  234.8 3.1 copy-start.2
  234.8 3.1 copy-start.4
  234.8 3.1 copy-start.8
  234.8 1.4 copy-start.14
  237.9 2.0 copy-start
  240.4 4.5 copy-start.1
  245.0 2.8 copy-start.3
  245.0 2.8 copy-start.5
  245.0 2.8 copy-start.9
  247.8 3.2 copy-start.2
  247.8 3.2 copy-start.4
  247.9 3.2 copy-start.8
  247.9 1.4 copy-start.14
  251.0 2.0 copy-start
  253.6 4.5 copy-start.1
  258.1 3.2 copy-start.3
  258.1 3.2 copy-start.5
  258.1 3.2 copy-start.9
  261.3 3.2 copy-start.2
  261.3 3.2 copy-start.4
  261.4 3.2 copy-start.8
  261.4 1.4 copy-start.14
  264.5 2.0 copy-start
  267.1 4.6 copy-start.1
  271.6 3.2 copy-start.3
  271.6 3.2 copy-start.5
  271.6 3.2 copy-start.9
  274.9 3.2 copy-start.2
  274.9 3.1 copy-start.4
  274.9 3.1 copy-start.8
  274.9 1.4 copy-start.14
  278.0 2.0 copy-start
  280.6 4.5 copy-start.1
  285.1 3.5 copy-start.3
  285.1 3.5 copy-start.5
  285.1 3.5 copy-start.9
  288.6 27.6 %copy-start.12 = (bf16[4,512,128]{2,1,0:T(8,128)(2,1)S(1)}, bf16[4,512,128]{2,1,0:T(8,128)(2,1)}, u32[]{:S(2)}) copy-start(bf16[4,512,128]{2,1,0:T(8,128)(2,1)} %get-tuple-element.122) | copy-start | bytes 1572868
  299.2 46.8 %copy-start.7 = (bf16[4,512,128]{2,1,0:T(8,128)(2,1)S(1)}, bf16[4,512,128]{2,1,0:T(8,128)(2,1)}, u32[]{:S(2)}) copy-start(bf16[4,512,128]{2,1,0:T(8,128)(2,1)} %copy-done.6) | copy-start | bytes 1572868
  311.7 25.1 %all-to-all-start.5 = ((bf16[16,2,8192]{2,1,0:T(2,128)(2,1)}), bf16[16,2,8192]{2,1,0:T(2,128)(2,1)S(1)}, u32[]{:S(2)}, u32[]{:S(2)}) async-start(bf16[16,2,8192]{2,1,0:T(2,128)(2,1)} %reshape.316), calls=%async_computation.5 | async-start | bytes 1048576 | tf_op jit(solution)/shard_map/all_to_all | solution.py:239
  336.8 35.4 %all-to-all-start.4 = ((bf16[16,2,8192]{2,1,0:T(2,128)(2,1)}), bf16[16,2,8192]{2,1,0:T(2,128)(2,1)S(1)}, u32[]{:S(2)}, u32[]{:S(2)}) async-start(bf16[16,2,8192]{2,1,0:T(2,128)(2,1)} %reshape.314), calls=%async_computation.4 | async-start | bytes 1048576 | tf_op jit(solution)/shard_map/all_to_all | solution.py:232
  345.9 202.8 %all-reduce.2.cloned.1.call-start = ((), (), s32[]{:S(2)}) async-start(), calls=%async_computation.9 | async-start | bytes 1572864 | tf_op jit(solution)/shard_map/psum | solution.py:256
  372.2 60.3 %copy-start.10 = (bf16[16,2,8192]{2,1,0:T(2,128)(2,1)}, bf16[16,2,8192]{2,1,0:T(2,128)(2,1)S(1)}, u32[]{:S(2)}) copy-start(bf16[16,2,8192]{2,1,0:T(2,128)(2,1)S(1)} %all-to-all-done.4) | copy-start | bytes 1572868
  372.2 191.2 %all-to-all-start.6 = ((bf16[16,2,8192]{2,1,0:T(2,128)(2,1)}), bf16[16,2,8192]{2,1,0:T(2,128)(2,1)}, u32[]{:S(2)}, u32[]{:S(2)}) async-start(bf16[16,2,8192]{2,1,0:T(2,128)(2,1)} %reshape.318), calls=%async_computation.6 | async-start | bytes 1048576 | tf_op jit(solution)/shard_map/all_to_all | solution.py:246
Sparse Core Ops, SparseCore 0:
  10.6 214.3 all-gather.4
  227.6 197.6 all-gather.2
  427.9 120.8 all-reduce.1
where the time goes:
time: 579 us; the launch traced here: 574 us
  waiting for transfers between devices  237 us (41%)
  local copies, waits for them, and re-layouts  98.4 us (17%)
  other arithmetic  95.4 us (16%)
  matrix products  76.4 us (13%)
  starting transfers between devices  50.4 us (9%)
  between operations  15.3 us (3%)
    psum x1, waiting for transfers between devices, local(): lax.psum(grad_weight.astype(jnp.bfloat16), 'dp').astype(jnp.float32)  116 us
    unnamed x9, other arithmetic  81.8 us
    all_gather x1, waiting for transfers between devices, local(): rows = lax.all_gather(cotangent, 'sp', axis=1, tiled=True)[0]  56.1 us
    all_gather x1, waiting for transfers between devices, local(): piece = lax.all_gather(out_weight, 'sp', axis=0, tiled=True)  43.7 us
    dot_general x9, matrix products, contract_first(): lax.dot_general(left, right, (((0,), (0,)), ((), ())), preferred_element_...  30.2 us
    unnamed x50, local copies, waits for them, and re-layouts  28 us
    dot_general x13, matrix products, contract_last(): lax.dot_general(left, right, (((1,), (1,)), ((), ())), preferred_element_...  25.5 us
    all_to_all x1, waiting for transfers between devices, local(): lax.all_to_all(value, 'sp', split_axis=2, concat_axis=1, tiled=True)  12.6 us
  transfers between devices with their start and end apart: 10, of which 6 were waited for; matrix products, arithmetic and copies ran while one was open for 44% of the time, Pallas kernels for 0%

commit v1 on v0

v1 whole, which is shorter than its diff:
```python
import functools

import jax
import jax.numpy as jnp
import numpy as np
from jax import lax
from jax.experimental import pallas as pl
from jax.experimental.pallas import tpu as pltpu
from jax.sharding import PartitionSpec as P

MESH = pl.DeviceIdType.MESH
BF = jnp.bfloat16
F32 = jnp.float32

HD = 128
HEADS = 16
CLIPS = 4
ROWS = 128
TOKENS = 2048
SLOT = TOKENS // CLIPS
D = 3072
HALF = D // 2
QB = 256
LOG2E = 1.4426950408889634
FACTOR = HD ** (-0.5)


def rotary_layout(head_dim):
    quarter = head_dim // 4
    rest_span = (head_dim - quarter) // 2
    part_spans = (quarter, rest_span, head_dim - quarter - rest_span)
    partner, signs, axis_of, frequency = [], [], [], []
    offset = 0
    for part_index in range(3):
        part_span = part_spans[part_index]
        half_span = part_span // 2
        for inner_dim in range(part_span):
            pair_index = inner_dim % half_span
            if inner_dim < half_span:
                partner.append(offset + inner_dim + half_span)
                signs.append(-1.0)
            else:
                partner.append(offset + inner_dim - half_span)
                signs.append(1.0)
            axis_of.append(part_index)
            frequency.append(10000.0 ** (-pair_index / half_span))
        offset += part_span
    return np.array(partner), np.array(signs), np.array(axis_of), np.array(frequency)


def partner_matrix():
    partner, signs, _, _ = rotary_layout(HD)
    matrix = np.zeros((HD, HD), np.float32)
    matrix[partner, np.arange(HD)] = signs
    return matrix


def nt(left, right):
    return lax.dot_general(left, right, (((1,), (1,)), ((), ())), preferred_element_type=F32)


def nn(left, right):
    return jnp.dot(left, right, preferred_element_type=F32)


def al(index, size):
    return pl.multiple_of(index, size)


def kernel(
    q_ref, k_ref, v_ref, cos_ref, sin_ref, perm_ref, w_ref, cot_ref, bucket_ref, cost_ref,
    mixed_out, gq_out, gk_out, gv_out, gw_out,
    rq, rk, qh, kh, vh, kt, vt, wbuf, probs, ot, rl, att, dealt, att_tok,
    gd, gdh, dot_t, dq_t, gsend, grecv, cot_t, ct, at_all, gw_send, xr, zs, zr,
    ssem, rsem,
):
    dp, sp = lax.axis_index("dp"), lax.axis_index("sp")
    y, xl, c = dp // 4, (dp // 2) % 2, dp % 2
    z, xh = sp // 2, sp % 2
    x = xh * 2 + xl

    def device(x_, y_, z_, c_):
        return (y_ * 4 + (x_ % 2) * 2 + c_, z_ * 2 + x_ // 2)

    def send(src, dst, s, r, to):
        pltpu.make_async_remote_copy(
            src_ref=src, dst_ref=dst, send_sem=ssem.at[s], recv_sem=rsem.at[r],
            device_id=to, device_id_type=MESH,
        ).start()

    def keep(src, dst, r):
        pltpu.make_async_copy(src, dst, rsem.at[r]).start()

    def wait(view, sem):
        pltpu.make_async_copy(view, view, sem).wait()

    barrier = pltpu.get_barrier_semaphore()

    def greet(to):
        pl.semaphore_signal(barrier, inc=1, device_id=to, device_id_type=MESH)

    @pl.loop(1, 16)
    def _(j):
        greet((dp, lax.rem(sp + j, 16)))

    @pl.loop(1, 8)
    def _(j):
        greet(device(x, (y + j // 2) % 4, z, (c + j) % 2))
        greet(device((x + j // 2) % 4, y, z, (c + j) % 2))

    pl.semaphore_wait(barrier, 29)

    def wblock(half, x_, y_):
        return wbuf.at[half, x_ // 2, :, y_, x_ % 2]

    piece = w_ref.at[pl.ds(al((y * 2 + xl) * 16, 16), 16), pl.ds(al(c * HALF, HALF), HALF)]
    spot = wbuf.at[c, xh, z, y, xl]
    keep(piece, spot, 8)

    @pl.loop(1, 8)
    def _(j):
        send(piece, spot, 8, 8, device(x, y, (z + j) % 8, c))

    cos, sin, perm = cos_ref[...], sin_ref[...], perm_ref[...]

    def turn(block, direction):
        return block.astype(F32) * cos + direction * nn(block, perm) * sin

    mine = pl.ds(al(sp * ROWS, ROWS), ROWS)
    lanes = lambda h: pl.ds(al(h * HD, HD), HD)

    for src, turned, dst, n in ((q_ref, rq, qh, 0), (k_ref, rk, kh, 1)):
        turned[sp] = turn(src[:, lanes(sp)], 1.0).astype(BF)
        keep(turned.at[sp], dst.at[mine], n)

        @pl.loop(1, 16)
        def _(j, src=src, turned=turned, dst=dst, n=n):
            h = lax.rem(sp + j, 16)
            turned[h] = turn(src[:, lanes(h)], 1.0).astype(BF)
            send(turned.at[h], dst.at[mine], n, n, (dp, h))

    keep(v_ref.at[:, lanes(sp)], vh.at[mine], 2)

    @pl.loop(1, 16)
    def _(j):
        h = lax.rem(sp + j, 16)
        send(v_ref.at[:, lanes(h)], vh.at[mine], 2, 2, (dp, h))

    def ring2(j):
        return (x + c * j) % 4, (y + (1 - c) * j) % 4

    def ring3(j):
        return (x + (1 - c) * j) % 4, (y + c * j) % 4

    def pass_on(i, x_, y_):
        block = wblock(c, x_, y_)
        send(block, block, 13, 13, device(x, y, z, 1 - c))
        for j in range(1, 4):
            tx, ty = ring3(j)
            send(block, block, 14, 17 + i * 3 + j - 1, device(tx, ty, z, c))

    own = wblock(c, x, y)
    wait(own, rsem.at[8])
    for j in range(1, 4):
        tx, ty = ring2(j)
        send(own, own, 9, 13 + j, device(tx, ty, z, c))
    pass_on(0, x, y)
    for j in range(1, 4):
        bx, by = ring2(4 - j)
        wait(wblock(c, bx, by), rsem.at[13 + j])
        pass_on(j, bx, by)

    wait(qh, rsem.at[0])
    wait(kh, rsem.at[1])
    wait(vh, rsem.at[2])
    kt[...] = kh[...].T
    vt[...] = vh[...].T
    narrow = jnp.where(bucket_ref[0] == 1, 0.0, -1e30).astype(F32)

    @pl.loop(0, TOKENS // QB)
    def _(b):
        cols = pl.ds(al(b * QB, QB), QB)
        slot = b // (SLOT // QB)
        scores = nt(kh[...], qh[cols, :]) * (FACTOR * LOG2E)
        parts = [
            scores[i * SLOT : (i + 1) * SLOT] + jnp.where(slot == i, 0.0, narrow)
            for i in range(CLIPS)
        ]
        scores = jnp.concatenate(parts, axis=0)
        top = jnp.max(scores, axis=0, keepdims=True)
        low = jnp.exp2(scores - top).astype(BF)
        probs[:, cols] = low
        scale = 1.0 / jnp.sum(low.astype(F32), axis=0, keepdims=True)
        rl[:, cols] = scale
        out = nn(vt[...], low) * scale
        ot[:, cols] = out
        att[cols, :] = out.T.astype(BF)

    costs = [cost_ref[0, k] for k in range(CLIPS)]
    wide = bucket_ref[0] == 1
    rank = []
    for k in range(CLIPS):
        count = jnp.int32(0)
        for j in range(CLIPS):
            if j != k:
                above = costs[j] >= costs[k] if j < k else costs[j] > costs[k]
                count = count + jnp.where(above, 1, 0)
        rank.append(jnp.where(wide, k, count))
    choose = [[jnp.where(rank[k] == r, 1.0, 0.0).astype(F32) for k in range(CLIPS)] for r in range(CLIPS)]

    slots = [att[k * SLOT : (k + 1) * SLOT, :].astype(F32) for k in range(CLIPS)]
    for r in range(CLIPS):
        picked = sum(slots[k] * choose[r][k] for k in range(CLIPS))
        dealt[r * SLOT : (r + 1) * SLOT, :] = picked.astype(BF)

    here = att_tok.at[xh, :, lanes(z)]
    keep(dealt.at[mine], here, 3)

    @pl.loop(1, 16)
    def _(j):
        t = lax.rem(sp + j, 16)
        send(dealt.at[pl.ds(al(t * ROWS, ROWS), ROWS)], here, 3, 3, (dp, t))

    for i in range(D // 128):
        cot_t[i * 128 : (i + 1) * 128, :] = cot_ref[:, i * 128 : (i + 1) * 128].T
    me8 = y * 2 + c
    ct_here = ct.at[:, lanes(me8)]
    keep(cot_t.at[pl.ds(al(y * 768, 768), 768)], ct_here, 10)

    @pl.loop(1, 8)
    def _(j):
        ty, tc = (y + j // 2) % 4, (c + j) % 2
        send(cot_t.at[pl.ds(al(ty * 768, 768), 768)], ct_here, 10, 10, device(x, ty, z, tc))

    for i in range(4):
        for j in range(1, 4):
            bx, by = ring2(4 - i) if i else (x, y)
            bx, by = (bx + (1 - c) * (4 - j)) % 4, (by + c * (4 - j)) % 4
            block = wblock(c, bx, by)
            wait(block, rsem.at[17 + i * 3 + j - 1])
            send(block, block, 13, 13, device(x, y, z, 1 - c))
    wait(wbuf.at[1 - c], rsem.at[13])

    def grad_of(h):
        first = wbuf[0, h % 2, h // 2].reshape(HD, HALF)
        second = wbuf[1, h % 2, h // 2].reshape(HD, HALF)
        gd[h] = (nt(cot_ref[:, :HALF], first) + nt(cot_ref[:, HALF:], second)).astype(BF)

    grad_of(sp)
    keep(gd.at[sp], gdh.at[mine], 4)

    @pl.loop(1, 16)
    def _(j):
        h = lax.rem(sp + j, 16)
        grad_of(h)
        send(gd.at[h], gdh.at[mine], 4, 4, (dp, h))

    wait(att_tok, rsem.at[3])
    at_here = at_all.at[pl.ds(al(me8 * ROWS, ROWS), ROWS)]
    keep(att_tok.at[c], at_here, 11)

    @pl.loop(1, 8)
    def _(j):
        ty, tc = (y + j // 2) % 4, (c + j) % 2
        send(att_tok.at[tc], at_here, 11, 11, device(x, ty, z, tc))

    for half in range(2):

        @pl.loop(0, HALF // 512)
        def _(i, half=half):
            cols = pl.ds(al(i * 512, 512), 512)
            total = nn(att_tok[0], wbuf[half, 0, :, :, :, :, cols].reshape(1024, 512))
            total += nn(att_tok[1], wbuf[half, 1, :, :, :, :, cols].reshape(1024, 512))
            mixed_out[:, pl.ds(al(half * HALF + i * 512, 512), 512)] = total.astype(BF)

    wait(gdh, rsem.at[4])
    slots = [gdh[k * SLOT : (k + 1) * SLOT, :].astype(F32) for k in range(CLIPS)]
    for k in range(CLIPS):
        picked = sum(slots[r] * choose[r][k] for r in range(CLIPS))
        dot_t[:, k * SLOT : (k + 1) * SLOT] = picked.T.astype(BF)

    def give(n, t):
        @pl.when(t == sp)
        def _():
            keep(gsend.at[n, t], grecv.at[n, sp], 5 + n)

        @pl.when(t != sp)
        def _():
            send(gsend.at[n, t], grecv.at[n, sp], 5 + n, 5 + n, (dp, t))

    scale = rl[...]
    scaled = (dot_t[...].astype(F32) * scale).astype(BF)
    centre = jnp.sum(dot_t[...].astype(F32) * ot[...], axis=0, keepdims=True)

    @pl.loop(0, TOKENS // QB)
    def _(i):
        b = (i + sp // 2) % (TOKENS // QB)
        rows = pl.ds(al(b * QB, QB), QB)
        low = probs[rows, :]
        value_grad = nt(low, scaled).astype(BF)
        gsend[0, b * 2] = value_grad[:ROWS]
        gsend[0, b * 2 + 1] = value_grad[ROWS:]
        give(0, b * 2)
        give(0, b * 2 + 1)

    scale = scale * FACTOR
    centre = centre * scale
    dq_t[...] = jnp.zeros_like(dq_t)

    @pl.loop(0, TOKENS // QB)
    def _(i):
        b = (i + sp // 2) % (TOKENS // QB)
        rows = pl.ds(al(b * QB, QB), QB)
        grad_probs = nn(vh[rows, :], dot_t[...])
        grad_scores = (probs[rows, :].astype(F32) * (grad_probs * scale - centre)).astype(BF)
        key_grad = nn(grad_scores, qh[...]).astype(BF)
        gsend[1, b * 2] = key_grad[:ROWS]
        gsend[1, b * 2 + 1] = key_grad[ROWS:]
        give(1, b * 2)
        give(1, b * 2 + 1)
        dq_t[...] += nn(kt[:, rows], grad_scores)

    @pl.loop(0, HEADS)
    def _(i):
        t = lax.rem(sp + i, 16)
        gsend[2, t] = dq_t[:, lanes(t)].T.astype(BF)
        give(2, t)

    wait(ct, rsem.at[10])
    wait(at_all, rsem.at[11])
    for b in range(4):
        gw_send[b] = nn(ct[b * 192 : (b + 1) * 192, :], at_all[...]).astype(BF)
        tx, tc = 2 * c + b // 2, b % 2
        same = jnp.logical_and(tx == x, tc == c)

        @pl.when(same)
        def _(b=b):
            keep(gw_send.at[b], xr.at[x], 12)

        @pl.when(jnp.logical_not(same))
        def _(b=b, tx=tx, tc=tc):
            send(gw_send.at[b], xr.at[x], 12, 12, device(tx, y, z, tc))

    wait(xr, rsem.at[12])
    for i in range(8):
        cols = slice(i * HD, (i + 1) * HD)
        total = sum(xr[j, :, cols].astype(F32) for j in range(4))
        zs[i] = total.astype(BF)
    keep(zs.at[z], zr.at[z], 9)

    @pl.loop(1, 8)
    def _(j):
        tz = (z + j) % 8
        send(zs.at[tz], zr.at[z], 15, 9, device(x, y, tz, c))

    wait(grecv.at[0], rsem.at[5])
    for h in range(HEADS):
        gv_out[:, h * HD : (h + 1) * HD] = grecv[0, h]

    for n, out in ((1, gk_out), (2, gq_out)):
        wait(grecv.at[n], rsem.at[5 + n])

        @pl.loop(0, HEADS)
        def _(h, n=n, out=out):
            out[:, lanes(h)] = turn(grecv[n, h], -1.0).astype(BF)

    wait(zr, rsem.at[9])
    gw_out[...] = sum(zr[i].astype(F32) for i in range(8))

    most = lambda ref: ref.at[pl.ds(0, 15)]
    wait(most(rq), ssem.at[0])
    wait(most(rk), ssem.at[1])
    wait(most(rk), ssem.at[2])
    wait(most(gd), ssem.at[3])
    wait(most(gd), ssem.at[4])
    for n in range(3):
        wait(most(gsend.at[n]), ssem.at[5 + n])
    wait(wbuf.at[0, 0, pl.ds(0, 7), 0, 0], ssem.at[8])
    wait(wbuf.at[c], ssem.at[13])
    wait(wbuf.at[0, 0, :, pl.ds(0, 3), 0], ssem.at[9])
    wait(wbuf.at[0, :, :, pl.ds(0, 3), :], ssem.at[14])
    wait(zs.at[pl.ds(0, 7)], ssem.at[15])
    wait(ct.at[:, pl.ds(0, 7 * HD)], ssem.at[10])
    wait(at_all.at[pl.ds(0, 7 * ROWS)], ssem.at[11])
    wait(gw_send.at[pl.ds(0, 3)], ssem.at[12])

    @pl.when(c != xh)
    def _():
        wait(gw_send.at[0], ssem.at[12])


def local(query, key_in, value, bucket, clip_cost, positions, out_weight, cotangent):
    _, _, axis_of, frequency = rotary_layout(HD)
    angles = jnp.transpose(positions[:, 0, :].astype(F32))
    angles = jnp.concatenate(
        [jnp.broadcast_to(angles[:, a : a + 1], (ROWS, int(np.sum(axis_of == a)))) for a in range(3)], axis=1
    ) * jnp.asarray(frequency, F32)
    perm = jnp.asarray(partner_matrix(), BF)

    vmem = pl.BlockSpec(memory_space=pltpu.VMEM)
    smem = pl.BlockSpec(memory_space=pltpu.SMEM)
    bf = lambda *shape: pltpu.VMEM(shape, BF)
    f32 = lambda *shape: pltpu.VMEM(shape, F32)
    shape = jax.ShapeDtypeStruct
    mixed, grad_query, grad_key, grad_value, grad_weight = pl.pallas_call(
        kernel,
        out_shape=(
            shape((ROWS, D), BF),
            shape((ROWS, TOKENS), BF),
            shape((ROWS, TOKENS), BF),
            shape((ROWS, TOKENS), BF),
            shape((192, HD), F32),
        ),
        in_specs=[vmem] * 8 + [smem] * 2,
        out_specs=(vmem,) * 5,
        scratch_shapes=[
            bf(16, ROWS, HD), bf(16, ROWS, HD),
            bf(TOKENS, HD), bf(TOKENS, HD), bf(TOKENS, HD),
            bf(HD, TOKENS), bf(HD, TOKENS),
            bf(2, 2, 8, 4, 2, 16, HALF),
            bf(TOKENS, TOKENS),
            f32(HD, TOKENS), f32(1, TOKENS),
            bf(TOKENS, HD), bf(TOKENS, HD),
            bf(2, ROWS, 1024),
            bf(16, ROWS, HD), bf(TOKENS, HD),
            bf(HD, TOKENS), f32(HD, TOKENS),
            bf(3, 16, ROWS, HD), bf(3, 16, ROWS, HD),
            bf(D, ROWS), bf(768, 1024), bf(1024, 1024),
            bf(4, 192, 1024), bf(4, 192, 1024),
            bf(8, 192, HD), bf(8, 192, HD),
            pltpu.SemaphoreType.DMA((16,)), pltpu.SemaphoreType.DMA((32,)),
        ],
        compiler_params=pltpu.CompilerParams(
            collective_id=0, has_side_effects=True, vmem_limit_bytes=62 * 2**20
        ),
    )(
        query[0], key_in[0], value[0], jnp.cos(angles), jnp.sin(angles), perm,
        out_weight, cotangent[0], bucket, clip_cost,
    )
    return mixed[None], grad_query[None], grad_key[None], grad_value[None], grad_weight.T


def solution(mesh):
    in_specs = (
        P("dp", "sp", None),
        P("dp", "sp", None),
        P("dp", "sp", None),
        P("dp"),
        P("dp", None),
        P(None, "dp", "sp"),
        P("sp", None),
        P("dp", "sp", None),
    )
    out_specs = (
        P("dp", "sp", None),
        P("dp", "sp", None),
        P("dp", "sp", None),
        P("dp", "sp", None),
        P("sp", "dp"),
    )
    return jax.shard_map(local, mesh=mesh, in_specs=in_specs, out_specs=out_specs, check_vma=False)
```

time: 579 us -> 169 us (0.29)
  waiting for transfers between devices: 237 us -> 0 us
  Pallas kernels: 0 us -> 158 us
  other arithmetic: 95.4 us -> 0.99 us
  local copies, waits for them, and re-layouts: 98.4 us -> 7.69 us
  matrix products: 76.4 us -> 0 us
  starting transfers between devices: 50.4 us -> 0 us
  between operations: 15.3 us -> 1.32 us
    pallas_call x0 -> x1, Pallas kernels: none -> 158 us  [local(): pl.pallas_call(kernel, out_shape=(shape((ROWS, D), BF), shape((ROWS, TOKE...]
    psum x1 -> x0, waiting for transfers between devices: 116 us -> none  [local(): lax.psum(grad_weight.astype(jnp.bfloat16), 'dp').astype(jnp.float32)]
    all_gather x2 -> x0, waiting for transfers between devices: 99.8 us -> none  [the longest x1 56.1 us: local(): rows = lax.all_gather(cotangent, 'sp', axis=1, tiled=True)[0]]
    unnamed x9 -> x0, other arithmetic: 81.8 us -> none
    dot_general x31 -> x0, matrix products: 76.4 us -> none  [the longest x9 30.2 us: contract_first(): lax.dot_general(left, right, (((0,), (0,)), ((), ())), preferred_element_...]
    all_to_all x7 -> x0, starting transfers between devices: 50.3 us -> none  [the longest x1 11.8 us: local(): lax.all_to_all(rot_query, 'sp', split_axis=2, concat_axis=1, tiled=True)]
    unnamed x50 -> x18, local copies, waits for them, and re-layouts: 28 us -> 7.46 us
    convert_element_type x8 -> x0, local copies, waits for them, and re-layouts: 20 us -> none  [the longest x1 8.66 us: local(): spin(query[0], cosine, sine_signed, 1.0, HD).astype(jnp.bfloat16)[None]]
  transfers between devices with their start and end apart: 10 -> 0, of which waited for: 6 -> 0; matrix products, arithmetic and copies ran while one was open for 44% -> 0% of each run, Pallas kernels for 0% -> 0%
where the time goes in v1:
time: 169 us; the launch traced here: 168 us
  Pallas kernels  158 us (93%)
  local copies, waits for them, and re-layouts  7.69 us (5%)
    pallas_call x1, Pallas kernels, local(): pl.pallas_call(kernel, out_shape=(shape((ROWS, D), BF), shape((ROWS, TOKE...  158 us
    unnamed x18, local copies, waits for them, and re-layouts  7.46 us

profile of v1, /device:TPU:1, one launch (start us, length us, event | category | flops | bytes accessed | tf_op | source)
XLA Modules:
  0.0 168.5 jit_solution(14012865089425988338)
XLA Ops:
  1.3 0.0 copy-start.4
  1.3 0.7 copy-done.4
  2.0 0.1 broadcast_in_dim.35
  2.1 0.1 broadcast_in_dim.39
  2.1 0.0 copy-start.5
  2.1 0.1 broadcast_in_dim.37
  2.2 0.6 copy-done.5
  2.8 1.0 fusion
  3.8 158.5 %shard_map.137 = (bf16[128,3072]{1,0:T(8,128)(2,1)}, bf16[128,2048]{1,0:T(8,128)(2,1)}, bf16[128,2048]{1,0:T(8,128)(2,1)}, bf16[128,2048]{1,0:T(8,128)(2,1)}, f32[192,128]{1,0:T(8,128)}) custom-call(bf16[128,2048]{1,0:T(8,128)(2,1)} %bitcast.25, bf16[128,2048]{1,0:T(8,128)(2,1)} %bitcast.26, bf16[128,2048]{1,0:T(8,128)(2,1)} %bitcast.27, ...), custom_call_target="tpu_custom_call" | custom-call | tf_op jit(solution)/shard_map/pallas_call | solution.py:405
  162.3 0.0 copy-start.2
  162.3 2.1 %copy.24 = bf16[1,128,3072]{2,1,0:T(8,128)(2,1)} copy(bf16[1,128,3072]{2,1,0:T(8,128)(2,1)} %bitcast.20) | data formatting | bytes 1572864
  164.4 0.0 copy-done.2
  164.4 0.0 copy-start.1
  164.4 0.8 copy.25
  165.2 0.4 copy-done.1
  165.6 0.0 copy-start
  165.6 0.8 copy.26
  166.4 0.4 copy-done
  166.9 0.0 copy-start.3
  166.9 0.8 copy.27
  167.7 0.2 copy-done.3
  167.8 0.6 copy.28
  (3 shorter events, 0.0 us)
Async XLA Ops:
  1.3 0.7 copy-start.4
  2.1 0.7 copy-start.5
  162.3 2.1 %copy-start.2 = (bf16[128,2048]{1,0:T(8,128)(2,1)S(1)}, bf16[128,2048]{1,0:T(8,128)(2,1)}, u32[]{:S(2)}) copy-start(bf16[128,2048]{1,0:T(8,128)(2,1)} %get-tuple-element.11) | copy-start | bytes 1572868
  164.4 1.2 copy-start.1
  165.6 1.2 copy-start
  166.9 1.0 copy-start.3

commit v2 on v1

--- a/solution.py
+++ b/solution.py
@@ -19,7 +19,9 @@
 TOKENS = 2048
 SLOT = TOKENS // CLIPS
 D = 3072
-HALF = D // 2
+PARTS = 2
+SPLIT = 1
+WIDE = D // PARTS
 QB = 256
 LOG2E = 1.4426950408889634
 FACTOR = HD ** (-0.5)
@@ -70,7 +72,7 @@
 def kernel(
     q_ref, k_ref, v_ref, cos_ref, sin_ref, perm_ref, w_ref, cot_ref, bucket_ref, cost_ref,
     mixed_out, gq_out, gk_out, gv_out, gw_out,
-    rq, rk, qh, kh, vh, kt, vt, wbuf, probs, ot, rl, att, dealt, att_tok,
+    rin, rel, qh, kh, vh, kt, vt, wbuf, probs, ot, rl, att, dealt, att_tok,
     gd, gdh, dot_t, dq_t, gsend, grecv, cot_t, ct, at_all, gw_send, xr, zs, zr,
     ssem, rsem,
 ):
@@ -110,16 +112,44 @@
 
     pl.semaphore_wait(barrier, 29)
 
-    def wblock(half, x_, y_):
-        return wbuf.at[half, x_ // 2, :, y_, x_ % 2]
-
-    piece = w_ref.at[pl.ds(al((y * 2 + xl) * 16, 16), 16), pl.ds(al(c * HALF, HALF), HALF)]
-    spot = wbuf.at[c, xh, z, y, xl]
-    keep(piece, spot, 8)
-
-    @pl.loop(1, 8)
-    def _(j):
-        send(piece, spot, 8, 8, device(x, y, (z + j) % 8, c))
+    def per_core(run):
+        @pl.when(c == 0)
+        def _():
+            run(0, pl.ds(0, SPLIT))
+
+        @pl.when(c == 1)
+        def _():
+            run(1, pl.ds(SPLIT, PARTS - SPLIT))
+
+    def give_piece(core, parts):
+        for t in range(parts.start, parts.start + parts.size):
+            piece = w_ref.at[pl.ds(al((y * 2 + xl) * 16, 16), 16), pl.ds(t * WIDE, WIDE)]
+            spot = wbuf.at[t, xh, z, y, xl]
+            keep(piece, spot, 8)
+
+            @pl.loop(1, 8)
+            def _(j, piece=piece, spot=spot):
+                send(piece, spot, 8, 8, device(x, y, (z + j) % 8, c))
+
+    per_core(give_piece)
+
+    lanes = lambda h: pl.ds(al(h * HD, HD), HD)
+    sibling = device(x, y, z, 1 - c)
+    me8 = y * 2 + c
+    for i in range(D // 128):
+        cot_t[i * 128 : (i + 1) * 128, :] = cot_ref[:, i * 128 : (i + 1) * 128].T
+    quarter = cot_t.at[pl.ds(al(y * 768, 768), 768)]
+    keep(quarter, ct.at[:, lanes(me8)], 10)
+    send(quarter, ct.at[:, lanes(me8)], 10, 10, sibling)
+    for j in range(1, 4):
+        ty = (y + j) % 4
+        send(cot_t.at[pl.ds(al(ty * 768, 768), 768)], ct.at[:, lanes(me8)], 10, 36 + j, device(x, ty, z, c))
+
+    def hand_over_cotangent():
+        for j in range(1, 4):
+            view = ct.at[:, lanes((y + 4 - j) % 4 * 2 + c)]
+            wait(view, rsem.at[36 + j])
+            send(view, view, 19, 10, sibling)
 
     cos, sin, perm = cos_ref[...], sin_ref[...], perm_ref[...]
 
@@ -127,58 +157,122 @@
         return block.astype(F32) * cos + direction * nn(block, perm) * sin
 
     mine = pl.ds(al(sp * ROWS, ROWS), ROWS)
-    lanes = lambda h: pl.ds(al(h * HD, HD), HD)
-
-    for src, turned, dst, n in ((q_ref, rq, qh, 0), (k_ref, rk, kh, 1)):
-        turned[sp] = turn(src[:, lanes(sp)], 1.0).astype(BF)
-        keep(turned.at[sp], dst.at[mine], n)
-
-        @pl.loop(1, 16)
-        def _(j, src=src, turned=turned, dst=dst, n=n):
-            h = lax.rem(sp + j, 16)
-            turned[h] = turn(src[:, lanes(h)], 1.0).astype(BF)
-            send(turned.at[h], dst.at[mine], n, n, (dp, h))
-
-    keep(v_ref.at[:, lanes(sp)], vh.at[mine], 2)
-
-    @pl.loop(1, 16)
-    def _(j):
-        h = lax.rem(sp + j, 16)
-        send(v_ref.at[:, lanes(h)], vh.at[mine], 2, 2, (dp, h))
-
-    def ring2(j):
-        return (x + c * j) % 4, (y + (1 - c) * j) % 4
-
-    def ring3(j):
-        return (x + (1 - c) * j) % 4, (y + c * j) % 4
-
-    def pass_on(i, x_, y_):
-        block = wblock(c, x_, y_)
-        send(block, block, 13, 13, device(x, y, z, 1 - c))
-        for j in range(1, 4):
-            tx, ty = ring3(j)
-            send(block, block, 14, 17 + i * 3 + j - 1, device(tx, ty, z, c))
-
-    own = wblock(c, x, y)
-    wait(own, rsem.at[8])
-    for j in range(1, 4):
-        tx, ty = ring2(j)
-        send(own, own, 9, 13 + j, device(tx, ty, z, c))
-    pass_on(0, x, y)
-    for j in range(1, 4):
-        bx, by = ring2(4 - j)
-        wait(wblock(c, bx, by), rsem.at[13 + j])
-        pass_on(j, bx, by)
+
+    partner = (dp, z * 2 + 1 - xh)
+    theirs = pl.ds(al(partner[1] * ROWS, ROWS), ROWS)
+
+    def fill(n, src, side):
+        @pl.loop(0, 8)
+        def _(i):
+            part = src[:, lanes(i * 2 + side)]
+            rin[n, side, i] = part if n == 2 else turn(part, 1.0).astype(BF)
+
+    def cross(n):
+        send(rin.at[n, 1 - xh], rel.at[n], 21 + n, 44 + n, partner)
+
+    def along(n, view, dst, rows, s):
+        keep(view.at[z], dst.at[rows], n)
+
+        @pl.loop(1, 8)
+        def _(j):
+            tz = lax.rem(z + j, 8)
+            send(view.at[tz], dst.at[rows], s, n, (dp, tz * 2 + xh))
+
+    arrays = ((0, q_ref, qh), (1, k_ref, kh), (2, v_ref, vh))
+
+    def hand_on(n, dst):
+        wait(rel.at[n], rsem.at[44 + n])
+        along(n, rel.at[n], dst, theirs, 24 + n)
+
+    for n, src, _ in arrays[:2]:
+        fill(n, src, 1 - xh)
+        cross(n)
+    for n, src, _ in arrays:
+        fill(n, src, xh)
+    fill(2, v_ref, 1 - xh)
+
+    def at(core, i, k):
+        return ((x + 8 + i) % 4, (y + 8 + k) % 4) if core else ((x + 8 + k) % 4, (y + 8 + i) % 4)
+
+    def block(core, parts, i, k):
+        bx, by = at(core, i, k)
+        return wbuf.at[parts, bx // 2, :, by, bx % 2]
+
+    def half_of(core, parts, i, k, m):
+        bx, by = at(core, i, k)
+        return wbuf.at[parts, bx // 2, pl.ds(4 * m, 4), by, bx % 2]
+
+    def ring_to(core, i, k):
+        return device(*at(core, i, k), z, c)
+
+    order = (0, -1, 1, 2)
+
+    def share(core, parts, n):
+        view = block(core, parts, order[n], 0)
+        send(view, view, 14, 21 + 4 * n, ring_to(core, 0, 1))
+        send(view, view, 14, 22 + 4 * n, ring_to(core, 0, -1))
+        send(view, view, 13, 13, sibling)
+
+    def pass_on(n):
+        def run(core, parts):
+            for side, m in ((-1, 0), (1, 1)):
+                view = block(core, parts, order[n], side)
+                part = half_of(core, parts, order[n], side, m)
+                wait(view, rsem.at[21 + 4 * n + m])
+                send(part, part, 15, 23 + 4 * n + m, ring_to(core, 0, -side))
+                send(view, view, 13, 13, sibling)
+
+        per_core(run)
+
+    def first_ring_start(core, parts):
+        own = block(core, parts, 0, 0)
+        wait(own, rsem.at[8])
+        send(own, own, 9, 17, ring_to(core, 1, 0))
+        send(own, own, 9, 18, ring_to(core, -1, 0))
+        share(core, parts, 0)
+
+    def first_ring(core, parts):
+        for n, side, m in ((1, -1, 0), (2, 1, 1)):
+            part = half_of(core, parts, side, 0, m)
+            wait(block(core, parts, side, 0), rsem.at[17 + m])
+            send(part, part, 16, 19 + m, ring_to(core, -side, 0))
+            share(core, parts, n)
+
+    def first_ring_end(core, parts):
+        for m in range(2):
+            wait(half_of(core, parts, 2, 0, m), rsem.at[19 + m])
+        share(core, parts, 3)
+
+    def second_ring_end(core, parts):
+        for n in range(4):
+            for m in range(2):
+                wait(half_of(core, parts, order[n], 2, m), rsem.at[23 + 4 * n + m])
+            view = block(core, parts, order[n], 2)
+            send(view, view, 13, 13, sibling)
+
+    def others_come(core, parts):
+        rest = pl.ds(0, SPLIT) if core else pl.ds(SPLIT, PARTS - SPLIT)
+        wait(wbuf.at[rest], rsem.at[13])
+
+    per_core(first_ring_start)
+    for n, _, dst in arrays[:2]:
+        along(n, rin.at[n, xh], dst, mine, n)
+    for n, _, dst in arrays[:2]:
+        hand_on(n, dst)
+    along(2, rin.at[2, xh], vh, mine, 2)
+    per_core(first_ring)
+    cross(2)
+    hand_over_cotangent()
+    pass_on(0)
+    per_core(first_ring_end)
+    hand_on(2, vh)
+    pass_on(1)
 
     wait(qh, rsem.at[0])
     wait(kh, rsem.at[1])
-    wait(vh, rsem.at[2])
-    kt[...] = kh[...].T
-    vt[...] = vh[...].T
     narrow = jnp.where(bucket_ref[0] == 1, 0.0, -1e30).astype(F32)
 
-    @pl.loop(0, TOKENS // QB)
-    def _(b):
+    def weigh(b):
         cols = pl.ds(al(b * QB, QB), QB)
         slot = b // (SLOT // QB)
         scores = nt(kh[...], qh[cols, :]) * (FACTOR * LOG2E)
@@ -192,7 +286,19 @@
         probs[:, cols] = low
         scale = 1.0 / jnp.sum(low.astype(F32), axis=0, keepdims=True)
         rl[:, cols] = scale
-        out = nn(vt[...], low) * scale
+
+    pl.loop(0, 4)(weigh)
+    pass_on(2)
+    pl.loop(4, TOKENS // QB)(weigh)
+    pass_on(3)
+
+    wait(vh, rsem.at[2])
+    vt[...] = vh[...].T
+
+    @pl.loop(0, TOKENS // QB)
+    def _(b):
+        cols = pl.ds(al(b * QB, QB), QB)
+        out = nn(vt[...], probs[:, cols]) * rl[:, cols]
         ot[:, cols] = out
         att[cols, :] = out.T.astype(BF)
 
@@ -221,30 +327,16 @@
         t = lax.rem(sp + j, 16)
         send(dealt.at[pl.ds(al(t * ROWS, ROWS), ROWS)], here, 3, 3, (dp, t))
 
-    for i in range(D // 128):
-        cot_t[i * 128 : (i + 1) * 128, :] = cot_ref[:, i * 128 : (i + 1) * 128].T
-    me8 = y * 2 + c
-    ct_here = ct.at[:, lanes(me8)]
-    keep(cot_t.at[pl.ds(al(y * 768, 768), 768)], ct_here, 10)
-
-    @pl.loop(1, 8)
-    def _(j):
-        ty, tc = (y + j // 2) % 4, (c + j) % 2
-        send(cot_t.at[pl.ds(al(ty * 768, 768), 768)], ct_here, 10, 10, device(x, ty, z, tc))
-
-    for i in range(4):
-        for j in range(1, 4):
-            bx, by = ring2(4 - i) if i else (x, y)
-            bx, by = (bx + (1 - c) * (4 - j)) % 4, (by + c * (4 - j)) % 4
-            block = wblock(c, bx, by)
-            wait(block, rsem.at[17 + i * 3 + j - 1])
-            send(block, block, 13, 13, device(x, y, z, 1 - c))
-    wait(wbuf.at[1 - c], rsem.at[13])
+    per_core(second_ring_end)
+
+    per_core(others_come)
 
     def grad_of(h):
-        first = wbuf[0, h % 2, h // 2].reshape(HD, HALF)
-        second = wbuf[1, h % 2, h // 2].reshape(HD, HALF)
-        gd[h] = (nt(cot_ref[:, :HALF], first) + nt(cot_ref[:, HALF:], second)).astype(BF)
+        total = sum(
+            nt(cot_ref[:, t * WIDE : (t + 1) * WIDE], wbuf[t, h % 2, h // 2].reshape(HD, WIDE))
+            for t in range(PARTS)
+        )
+        gd[h] = total.astype(BF)
 
     grad_of(sp)
     keep(gd.at[sp], gdh.at[mine], 4)
@@ -256,22 +348,33 @@
         send(gd.at[h], gdh.at[mine], 4, 4, (dp, h))
 
     wait(att_tok, rsem.at[3])
-    at_here = at_all.at[pl.ds(al(me8 * ROWS, ROWS), ROWS)]
+    def rows_of(ty, tc, first=0, count=ROWS):
+        return at_all.at[pl.ds(al((ty * 2 + tc) * ROWS + first, count), count)]
+
+    at_here = rows_of(y, c)
     keep(att_tok.at[c], at_here, 11)
-
-    @pl.loop(1, 8)
-    def _(j):
-        ty, tc = (y + j // 2) % 4, (c + j) % 2
-        send(att_tok.at[tc], at_here, 11, 11, device(x, ty, z, tc))
-
-    for half in range(2):
-
-        @pl.loop(0, HALF // 512)
-        def _(i, half=half):
+    for tc in range(2):
+        send(att_tok.at[tc], at_here, 11, 40 + c, device(x, (y + 1) % 4, z, tc))
+        send(att_tok.at[tc], at_here, 11, 42 + c, device(x, (y + 3) % 4, z, tc))
+    send(att_tok.at[1 - c], at_here, 11, 11, sibling)
+
+    for t in range(PARTS):
+
+        @pl.loop(0, WIDE // 512)
+        def _(i, t=t):
             cols = pl.ds(al(i * 512, 512), 512)
-            total = nn(att_tok[0], wbuf[half, 0, :, :, :, :, cols].reshape(1024, 512))
-            total += nn(att_tok[1], wbuf[half, 1, :, :, :, :, cols].reshape(1024, 512))
-            mixed_out[:, pl.ds(al(half * HALF + i * 512, 512), 512)] = total.astype(BF)
+            total = nn(att_tok[0], wbuf[t, 0, :, :, :, :, cols].reshape(1024, 512))
+            total += nn(att_tok[1], wbuf[t, 1, :, :, :, :, cols].reshape(1024, 512))
+            mixed_out[:, pl.ds(al(t * WIDE + i * 512, 512), 512)] = total.astype(BF)
+
+    for m, step in ((0, 3), (1, 1)):
+        ty = (y + step) % 4
+        for tc in range(2):
+            wait(rows_of(ty, tc), rsem.at[40 + 2 * m + tc])
+            part = rows_of(ty, tc, 64 * m, 64)
+            send(part, part, 18, 11, device(x, (y + 4 - step) % 4, z, c))
+
+    kt[...] = kh[...].T
 
     wait(gdh, rsem.at[4])
     slots = [gdh[k * SLOT : (k + 1) * SLOT, :].astype(F32) for k in range(CLIPS)]
@@ -302,6 +405,21 @@
         gsend[0, b * 2 + 1] = value_grad[ROWS:]
         give(0, b * 2)
         give(0, b * 2 + 1)
+
+    wait(ct.at[:, pl.ds(0, 5 * HD)], rsem.at[10])
+    wait(at_all.at[pl.ds(0, 4 * ROWS)], rsem.at[11])
+    for b in range(4):
+        gw_send[b] = nn(ct[b * 192 : (b + 1) * 192, :], at_all[...]).astype(BF)
+        tx, tc = 2 * c + b // 2, b % 2
+        same = jnp.logical_and(tx == x, tc == c)
+
+        @pl.when(same)
+        def _(b=b):
+            keep(gw_send.at[b], xr.at[x], 12)
+
+        @pl.when(jnp.logical_not(same))
+        def _(b=b, tx=tx, tc=tc):
+            send(gw_send.at[b], xr.at[x], 12, 12, device(tx, y, z, tc))
 
     scale = scale * FACTOR
     centre = centre * scale
@@ -326,21 +444,6 @@
         gsend[2, t] = dq_t[:, lanes(t)].T.astype(BF)
         give(2, t)
 
-    wait(ct, rsem.at[10])
-    wait(at_all, rsem.at[11])
-    for b in range(4):
-        gw_send[b] = nn(ct[b * 192 : (b + 1) * 192, :], at_all[...]).astype(BF)
-        tx, tc = 2 * c + b // 2, b % 2
-        same = jnp.logical_and(tx == x, tc == c)
-
-        @pl.when(same)
-        def _(b=b):
-            keep(gw_send.at[b], xr.at[x], 12)
-
-        @pl.when(jnp.logical_not(same))
-        def _(b=b, tx=tx, tc=tc):
-            send(gw_send.at[b], xr.at[x], 12, 12, device(tx, y, z, tc))
-
     wait(xr, rsem.at[12])
     for i in range(8):
         cols = slice(i * HD, (i + 1) * HD)
@@ -351,7 +454,7 @@
     @pl.loop(1, 8)
     def _(j):
         tz = (z + j) % 8
-        send(zs.at[tz], zr.at[z], 15, 9, device(x, y, tz, c))
+        send(zs.at[tz], zr.at[z], 17, 9, device(x, y, tz, c))
 
     wait(grecv.at[0], rsem.at[5])
     for h in range(HEADS):
@@ -368,20 +471,29 @@
     gw_out[...] = sum(zr[i].astype(F32) for i in range(8))
 
     most = lambda ref: ref.at[pl.ds(0, 15)]
-    wait(most(rq), ssem.at[0])
-    wait(most(rk), ssem.at[1])
-    wait(most(rk), ssem.at[2])
+    for n in range(3):
+        wait(rel.at[n, pl.ds(0, 7)], ssem.at[n])
+        wait(rel.at[n], ssem.at[21 + n])
+        wait(rel.at[n, pl.ds(0, 7)], ssem.at[24 + n])
     wait(most(gd), ssem.at[3])
     wait(most(gd), ssem.at[4])
     for n in range(3):
         wait(most(gsend.at[n]), ssem.at[5 + n])
-    wait(wbuf.at[0, 0, pl.ds(0, 7), 0, 0], ssem.at[8])
-    wait(wbuf.at[c], ssem.at[13])
-    wait(wbuf.at[0, 0, :, pl.ds(0, 3), 0], ssem.at[9])
-    wait(wbuf.at[0, :, :, pl.ds(0, 3), :], ssem.at[14])
-    wait(zs.at[pl.ds(0, 7)], ssem.at[15])
-    wait(ct.at[:, pl.ds(0, 7 * HD)], ssem.at[10])
-    wait(at_all.at[pl.ds(0, 7 * ROWS)], ssem.at[11])
+
+    def weights_left(core, parts):
+        wait(wbuf.at[parts, 0, pl.ds(0, 7), 0, 0], ssem.at[8])
+        wait(wbuf.at[parts], ssem.at[13])
+        wait(wbuf.at[parts, 0, :, 0, :], ssem.at[9])
+        wait(wbuf.at[parts, 0, :, 0, 0], ssem.at[16])
+        wait(wbuf.at[parts, 0], ssem.at[14])
+        wait(wbuf.at[parts, 0, :, :, 0], ssem.at[15])
+
+    per_core(weights_left)
+    wait(zs.at[pl.ds(0, 7)], ssem.at[17])
+    wait(ct.at[:, pl.ds(0, 4 * HD)], ssem.at[10])
+    wait(ct.at[:, pl.ds(0, 3 * HD)], ssem.at[19])
+    wait(at_all.at[pl.ds(0, 5 * ROWS)], ssem.at[11])
+    wait(at_all.at[pl.ds(0, 2 * ROWS)], ssem.at[18])
     wait(gw_send.at[pl.ds(0, 3)], ssem.at[12])
 
     @pl.when(c != xh)
@@ -414,10 +526,10 @@
         in_specs=[vmem] * 8 + [smem] * 2,
         out_specs=(vmem,) * 5,
         scratch_shapes=[
-            bf(16, ROWS, HD), bf(16, ROWS, HD),
+            bf(3, 2, 8, ROWS, HD), bf(3, 8, ROWS, HD),
             bf(TOKENS, HD), bf(TOKENS, HD), bf(TOKENS, HD),
             bf(HD, TOKENS), bf(HD, TOKENS),
-            bf(2, 2, 8, 4, 2, 16, HALF),
+            bf(PARTS, 2, 8, 4, 2, 16, WIDE),
             bf(TOKENS, TOKENS),
             f32(HD, TOKENS), f32(1, TOKENS),
             bf(TOKENS, HD), bf(TOKENS, HD),
@@ -428,7 +540,7 @@
             bf(D, ROWS), bf(768, 1024), bf(1024, 1024),
             bf(4, 192, 1024), bf(4, 192, 1024),
             bf(8, 192, HD), bf(8, 192, HD),
-            pltpu.SemaphoreType.DMA((16,)), pltpu.SemaphoreType.DMA((32,)),
+            pltpu.SemaphoreType.DMA((27,)), pltpu.SemaphoreType.DMA((47,)),
         ],
         compiler_params=pltpu.CompilerParams(
             collective_id=0, has_side_effects=True, vmem_limit_bytes=62 * 2**20

time: 169 us -> 151 us (0.89)
  Pallas kernels: 158 us -> 140 us
    pallas_call x1, Pallas kernels: 158 us -> 140 us  [local(): pl.pallas_call(kernel, out_shape=(shape((ROWS, D), BF), shape((ROWS, TOKE...]
where the time goes in v2:
time: 151 us; the launch traced here: 150 us
  Pallas kernels  140 us (93%)
  local copies, waits for them, and re-layouts  7.69 us (5%)
    pallas_call x1, Pallas kernels, local(): pl.pallas_call(kernel, out_shape=(shape((ROWS, D), BF), shape((ROWS, TOKE...  140 us
    unnamed x18, local copies, waits for them, and re-layouts  7.46 us

profile of v2, /device:TPU:1, one launch (start us, length us, event | category | flops | bytes accessed | tf_op | source)
XLA Modules:
  0.0 150.4 jit_solution(9167276961075274485)
XLA Ops:
  1.3 0.0 copy-start.4
  1.3 0.7 copy-done.4
  2.0 0.1 broadcast_in_dim.35
  2.1 0.1 broadcast_in_dim.39
  2.1 0.0 copy-start.5
  2.1 0.1 broadcast_in_dim.37
  2.2 0.6 copy-done.5
  2.8 1.0 fusion
  3.8 140.4 %shard_map.137 = (bf16[128,3072]{1,0:T(8,128)(2,1)}, bf16[128,2048]{1,0:T(8,128)(2,1)}, bf16[128,2048]{1,0:T(8,128)(2,1)}, bf16[128,2048]{1,0:T(8,128)(2,1)}, f32[192,128]{1,0:T(8,128)}) custom-call(bf16[128,2048]{1,0:T(8,128)(2,1)} %bitcast.25, bf16[128,2048]{1,0:T(8,128)(2,1)} %bitcast.26, bf16[128,2048]{1,0:T(8,128)(2,1)} %bitcast.27, ...), custom_call_target="tpu_custom_call" | custom-call | tf_op jit(solution)/shard_map/pallas_call | solution.py:517
  144.2 0.0 copy-start.2
  144.2 2.1 %copy.24 = bf16[1,128,3072]{2,1,0:T(8,128)(2,1)} copy(bf16[1,128,3072]{2,1,0:T(8,128)(2,1)} %bitcast.20) | data formatting | bytes 1572864
  146.4 0.0 copy-done.2
  146.4 0.0 copy-start.1
  146.4 0.8 copy.25
  147.2 0.4 copy-done.1
  147.6 0.0 copy-start
  147.6 0.8 copy.26
  148.4 0.4 copy-done
  148.8 0.0 copy-start.3
  148.8 0.8 copy.27
  149.6 0.2 copy-done.3
  149.8 0.6 copy.28
  (3 shorter events, 0.0 us)
Async XLA Ops:
  1.3 0.7 copy-start.4
  2.1 0.7 copy-start.5
  144.2 2.1 %copy-start.2 = (bf16[128,2048]{1,0:T(8,128)(2,1)S(1)}, bf16[128,2048]{1,0:T(8,128)(2,1)}, u32[]{:S(2)}) copy-start(bf16[128,2048]{1,0:T(8,128)(2,1)} %get-tuple-element.11) | copy-start | bytes 1572868
  146.4 1.2 copy-start.1
  147.6 1.2 copy-start
  148.8 1.0 copy-start.3

commit v3 on v2

--- a/solution.py
+++ b/solution.py
@@ -25,6 +25,7 @@
 QB = 256
 LOG2E = 1.4426950408889634
 FACTOR = HD ** (-0.5)
+SCALE = FACTOR * LOG2E
 
 
 def rotary_layout(head_dim):
@@ -69,12 +70,31 @@
     return pl.multiple_of(index, size)
 
 
+def finish(mixed_ref, gk_ref, gv_ref, gq_ref, zr_ref, cos_ref, sin_ref, perm_ref, mixed_out, gq_out, gk_out, gv_out, gw_out, wide, keys, values, sems):
+    ways = ((mixed_ref, wide, mixed_out), (gk_ref, keys, gk_out), (gv_ref, values, gv_out))
+    loads = [pltpu.make_async_copy(src, held, sems.at[i]) for i, (src, held, _) in enumerate(ways)]
+    stores = [pltpu.make_async_copy(held, dst, sems.at[3 + i]) for i, (_, held, dst) in enumerate(ways)]
+    for load in loads:
+        load.start()
+    for load, store in zip(loads, stores):
+        load.wait()
+        store.start()
+    for h in range(HEADS):
+        part = gq_ref[h]
+        turned = part.astype(F32) * cos_ref[...] - nn(part, perm_ref[...]) * sin_ref[...]
+        gq_out[:, h * HD : (h + 1) * HD] = turned.astype(BF)
+    gw_out[...] = sum(zr_ref[i].astype(F32) for i in range(8))
+    for store in stores:
+        store.wait()
+
+
 def kernel(
-    q_ref, k_ref, v_ref, cos_ref, sin_ref, perm_ref, w_ref, cot_ref, bucket_ref, cost_ref,
-    mixed_out, gq_out, gk_out, gv_out, gw_out,
+    q_hbm, k_hbm, v_hbm, cos_ref, sin_ref, perm_ref, w_hbm, cot_hbm, bucket_ref, cost_ref,
+    mixed_hbm, gk_hbm, gv_hbm, gq_hbm, zr_hbm,
+    q_ref, k_ref, v_ref, cot_ref, mixed_out, gk_out, gv_out,
     rin, rel, qh, kh, vh, kt, vt, wbuf, probs, ot, rl, att, dealt, att_tok,
     gd, gdh, dot_t, dq_t, gsend, grecv, cot_t, ct, at_all, gw_send, xr, zs, zr,
-    ssem, rsem,
+    ssem, rsem, lsem,
 ):
     dp, sp = lax.axis_index("dp"), lax.axis_index("sp")
     y, xl, c = dp // 4, (dp // 2) % 2, dp % 2
@@ -96,6 +116,13 @@
     def wait(view, sem):
         pltpu.make_async_copy(view, view, sem).wait()
 
+    loads = [
+        pltpu.make_async_copy(src, dst, lsem.at[i])
+        for i, (src, dst) in enumerate(((cot_hbm, cot_ref), (q_hbm, q_ref), (k_hbm, k_ref), (v_hbm, v_ref)))
+    ]
+    for load in loads:
+        load.start()
+
     barrier = pltpu.get_barrier_semaphore()
 
     def greet(to):
@@ -123,7 +150,7 @@
 
     def give_piece(core, parts):
         for t in range(parts.start, parts.start + parts.size):
-            piece = w_ref.at[pl.ds(al((y * 2 + xl) * 16, 16), 16), pl.ds(t * WIDE, WIDE)]
+            piece = w_hbm.at[pl.ds(al((y * 2 + xl) * 16, 16), 16), pl.ds(t * WIDE, WIDE)]
             spot = wbuf.at[t, xh, z, y, xl]
             keep(piece, spot, 8)
 
@@ -136,6 +163,7 @@
     lanes = lambda h: pl.ds(al(h * HD, HD), HD)
     sibling = device(x, y, z, 1 - c)
     me8 = y * 2 + c
+    loads[0].wait()
     for i in range(D // 128):
         cot_t[i * 128 : (i + 1) * 128, :] = cot_ref[:, i * 128 : (i + 1) * 128].T
     quarter = cot_t.at[pl.ds(al(y * 768, 768), 768)]
@@ -185,10 +213,14 @@
         along(n, rel.at[n], dst, theirs, 24 + n)
 
     for n, src, _ in arrays[:2]:
+        loads[1 + n].wait()
         fill(n, src, 1 - xh)
         cross(n)
-    for n, src, _ in arrays:
-        fill(n, src, xh)
+    fill(0, q_ref, xh)
+    along(0, rin.at[0, xh], qh, mine, 0)
+    fill(1, k_ref, xh)
+    loads[3].wait()
+    fill(2, v_ref, xh)
     fill(2, v_ref, 1 - xh)
 
     def at(core, i, k):
@@ -255,8 +287,7 @@
         wait(wbuf.at[rest], rsem.at[13])
 
     per_core(first_ring_start)
-    for n, _, dst in arrays[:2]:
-        along(n, rin.at[n, xh], dst, mine, n)
+    along(1, rin.at[1, xh], kh, mine, 1)
     for n, _, dst in arrays[:2]:
         hand_on(n, dst)
     along(2, rin.at[2, xh], vh, mine, 2)
@@ -275,17 +306,14 @@
     def weigh(b):
         cols = pl.ds(al(b * QB, QB), QB)
         slot = b // (SLOT // QB)
-        scores = nt(kh[...], qh[cols, :]) * (FACTOR * LOG2E)
-        parts = [
-            scores[i * SLOT : (i + 1) * SLOT] + jnp.where(slot == i, 0.0, narrow)
-            for i in range(CLIPS)
-        ]
-        scores = jnp.concatenate(parts, axis=0)
-        top = jnp.max(scores, axis=0, keepdims=True)
-        low = jnp.exp2(scores - top).astype(BF)
-        probs[:, cols] = low
-        scale = 1.0 / jnp.sum(low.astype(F32), axis=0, keepdims=True)
-        rl[:, cols] = scale
+        scores = nt(kh[...], qh[cols, :])
+        parts = [scores[i * SLOT : (i + 1) * SLOT] for i in range(CLIPS)]
+        masks = [jnp.where(slot == i, 0.0, narrow) for i in range(CLIPS)]
+        tops = [jnp.max(part, axis=0, keepdims=True) + mask for part, mask in zip(parts, masks)]
+        top = functools.reduce(jnp.maximum, tops) * SCALE
+        for i in range(CLIPS):
+            low = jnp.exp2(parts[i] * SCALE - (top - masks[i])).astype(BF)
+            probs[i * SLOT : (i + 1) * SLOT, cols] = low
 
     pl.loop(0, 4)(weigh)
     pass_on(2)
@@ -293,12 +321,16 @@
     pass_on(3)
 
     wait(vh, rsem.at[2])
-    vt[...] = vh[...].T
+    vt[:HD, :] = vh[...].T
+    vt[HD:, :] = jnp.ones((16, TOKENS), BF)
 
     @pl.loop(0, TOKENS // QB)
     def _(b):
         cols = pl.ds(al(b * QB, QB), QB)
-        out = nn(vt[...], probs[:, cols]) * rl[:, cols]
+        out = nn(vt[...], probs[:, cols])
+        scale = 1.0 / out[HD : HD + 1]
+        rl[:, cols] = scale
+        out = out[:HD] * scale
         ot[:, cols] = out
         att[cols, :] = out.T.astype(BF)
 
@@ -367,6 +399,14 @@
             total += nn(att_tok[1], wbuf[t, 1, :, :, :, :, cols].reshape(1024, 512))
             mixed_out[:, pl.ds(al(t * WIDE + i * 512, 512), 512)] = total.astype(BF)
 
+    stores = [
+        pltpu.make_async_copy(src, dst, lsem.at[4 + i])
+        for i, (src, dst) in enumerate(
+            ((mixed_out, mixed_hbm), (gv_out, gv_hbm), (gk_out, gk_hbm), (grecv.at[2], gq_hbm), (zr, zr_hbm))
+        )
+    ]
+    stores[0].start()
+
     for m, step in ((0, 3), (1, 1)):
         ty = (y + step) % 4
         for tc in range(2):
@@ -380,7 +420,8 @@
     slots = [gdh[k * SLOT : (k + 1) * SLOT, :].astype(F32) for k in range(CLIPS)]
     for k in range(CLIPS):
         picked = sum(slots[r] * choose[r][k] for r in range(CLIPS))
-        dot_t[:, k * SLOT : (k + 1) * SLOT] = picked.T.astype(BF)
+        part = slice(k * SLOT, (k + 1) * SLOT)
+        dot_t[:, part] = (picked.T * rl[:, part]).astype(BF)
 
     def give(n, t):
         @pl.when(t == sp)
@@ -391,8 +432,6 @@
         def _():
             send(gsend.at[n, t], grecv.at[n, sp], 5 + n, 5 + n, (dp, t))
 
-    scale = rl[...]
-    scaled = (dot_t[...].astype(F32) * scale).astype(BF)
     centre = jnp.sum(dot_t[...].astype(F32) * ot[...], axis=0, keepdims=True)
 
     @pl.loop(0, TOKENS // QB)
@@ -400,7 +439,7 @@
         b = (i + sp // 2) % (TOKENS // QB)
         rows = pl.ds(al(b * QB, QB), QB)
         low = probs[rows, :]
-        value_grad = nt(low, scaled).astype(BF)
+        value_grad = nt(low, dot_t[...]).astype(BF)
         gsend[0, b * 2] = value_grad[:ROWS]
         gsend[0, b * 2 + 1] = value_grad[ROWS:]
         give(0, b * 2)
@@ -421,8 +460,6 @@
         def _(b=b, tx=tx, tc=tc):
             send(gw_send.at[b], xr.at[x], 12, 12, device(tx, y, z, tc))
 
-    scale = scale * FACTOR
-    centre = centre * scale
     dq_t[...] = jnp.zeros_like(dq_t)
 
     @pl.loop(0, TOKENS // QB)
@@ -430,8 +467,8 @@
         b = (i + sp // 2) % (TOKENS // QB)
         rows = pl.ds(al(b * QB, QB), QB)
         grad_probs = nn(vh[rows, :], dot_t[...])
-        grad_scores = (probs[rows, :].astype(F32) * (grad_probs * scale - centre)).astype(BF)
-        key_grad = nn(grad_scores, qh[...]).astype(BF)
+        grad_scores = (probs[rows, :].astype(F32) * (grad_probs - centre)).astype(BF)
+        key_grad = (nn(grad_scores, qh[...]) * FACTOR).astype(BF)
         gsend[1, b * 2] = key_grad[:ROWS]
         gsend[1, b * 2 + 1] = key_grad[ROWS:]
         give(1, b * 2)
@@ -441,7 +478,7 @@
     @pl.loop(0, HEADS)
     def _(i):
         t = lax.rem(sp + i, 16)
-        gsend[2, t] = dq_t[:, lanes(t)].T.astype(BF)
+        gsend[2, t] = (dq_t[:, lanes(t)].T * FACTOR).astype(BF)
         give(2, t)
 
     wait(xr, rsem.at[12])
@@ -459,17 +496,21 @@
     wait(grecv.at[0], rsem.at[5])
     for h in range(HEADS):
         gv_out[:, h * HD : (h + 1) * HD] = grecv[0, h]
-
-    for n, out in ((1, gk_out), (2, gq_out)):
-        wait(grecv.at[n], rsem.at[5 + n])
-
-        @pl.loop(0, HEADS)
-        def _(h, n=n, out=out):
-            out[:, lanes(h)] = turn(grecv[n, h], -1.0).astype(BF)
-
+    stores[1].start()
+    wait(grecv.at[1], rsem.at[6])
+
+    @pl.loop(0, HEADS)
+    def _(h):
+        gk_out[:, lanes(h)] = turn(grecv[1, h], -1.0).astype(BF)
+
+    stores[2].start()
     wait(zr, rsem.at[9])
-    gw_out[...] = sum(zr[i].astype(F32) for i in range(8))
-
+    stores[4].start()
+    wait(grecv.at[2], rsem.at[7])
+    stores[3].start()
+
+    for store in stores:
+        store.wait()
     most = lambda ref: ref.at[pl.ds(0, 15)]
     for n in range(3):
         wait(rel.at[n, pl.ds(0, 7)], ssem.at[n])
@@ -514,21 +555,20 @@
     bf = lambda *shape: pltpu.VMEM(shape, BF)
     f32 = lambda *shape: pltpu.VMEM(shape, F32)
     shape = jax.ShapeDtypeStruct
-    mixed, grad_query, grad_key, grad_value, grad_weight = pl.pallas_call(
+    hbm = pl.BlockSpec(memory_space=pl.ANY)
+    cos, sin = jnp.cos(angles), jnp.sin(angles)
+    rows = shape((ROWS, TOKENS), BF)
+    mixed, grad_key, grad_value, raw_query, terms = pl.pallas_call(
         kernel,
-        out_shape=(
-            shape((ROWS, D), BF),
-            shape((ROWS, TOKENS), BF),
-            shape((ROWS, TOKENS), BF),
-            shape((ROWS, TOKENS), BF),
-            shape((192, HD), F32),
-        ),
-        in_specs=[vmem] * 8 + [smem] * 2,
-        out_specs=(vmem,) * 5,
+        out_shape=(shape((ROWS, D), BF), rows, rows, shape((16, ROWS, HD), BF), shape((8, 192, HD), BF)),
+        in_specs=[hbm] * 3 + [vmem] * 3 + [hbm] * 2 + [smem] * 2,
+        out_specs=(hbm,) * 5,
         scratch_shapes=[
+            bf(ROWS, TOKENS), bf(ROWS, TOKENS), bf(ROWS, TOKENS), bf(ROWS, D),
+            bf(ROWS, D), bf(ROWS, TOKENS), bf(ROWS, TOKENS),
             bf(3, 2, 8, ROWS, HD), bf(3, 8, ROWS, HD),
             bf(TOKENS, HD), bf(TOKENS, HD), bf(TOKENS, HD),
-            bf(HD, TOKENS), bf(HD, TOKENS),
+            bf(HD, TOKENS), bf(HD + 16, TOKENS),
             bf(PARTS, 2, 8, 4, 2, 16, WIDE),
             bf(TOKENS, TOKENS),
             f32(HD, TOKENS), f32(1, TOKENS),
@@ -540,15 +580,22 @@
             bf(D, ROWS), bf(768, 1024), bf(1024, 1024),
             bf(4, 192, 1024), bf(4, 192, 1024),
             bf(8, 192, HD), bf(8, 192, HD),
-            pltpu.SemaphoreType.DMA((27,)), pltpu.SemaphoreType.DMA((47,)),
+            pltpu.SemaphoreType.DMA((27,)), pltpu.SemaphoreType.DMA((47,)), pltpu.SemaphoreType.DMA((9,)),
         ],
         compiler_params=pltpu.CompilerParams(
             collective_id=0, has_side_effects=True, vmem_limit_bytes=62 * 2**20
         ),
     )(
-        query[0], key_in[0], value[0], jnp.cos(angles), jnp.sin(angles), perm,
+        query[0], key_in[0], value[0], cos, sin, perm,
         out_weight, cotangent[0], bucket, clip_cost,
     )
+    mixed, grad_query, grad_key, grad_value, grad_weight = pl.pallas_call(
+        finish,
+        out_shape=(shape((ROWS, D), BF), rows, rows, rows, shape((192, HD), F32)),
+        in_specs=[hbm] * 3 + [vmem] * 5,
+        out_specs=(hbm, vmem, hbm, hbm, vmem),
+        scratch_shapes=[bf(ROWS, D), bf(ROWS, TOKENS), bf(ROWS, TOKENS), pltpu.SemaphoreType.DMA((6,))],
+    )(mixed, grad_key, grad_value, raw_query, terms, cos, sin, perm)
     return mixed[None], grad_query[None], grad_key[None], grad_value[None], grad_weight.T
 
 

time: 151 us -> 144 us (0.954)
  local copies, waits for them, and re-layouts: 7.69 us -> 1.5 us
    unnamed x18 -> x5, local copies, waits for them, and re-layouts: 7.46 us -> 1.27 us
    pallas_call x1 -> x2, Pallas kernels: 140 us -> 139 us  [the longest x1 135 us: local(): pl.pallas_call(kernel, out_shape=(shape((ROWS, D), BF), rows, rows, shape...]
where the time goes in v3:
time: 144 us; the launch traced here: 143 us
  Pallas kernels  139 us (97%)
  local copies, waits for them, and re-layouts  1.5 us (1%)
    pallas_call x1, Pallas kernels, local(): pl.pallas_call(kernel, out_shape=(shape((ROWS, D), BF), rows, rows, shape...  135 us
    pallas_call x1, Pallas kernels, local(): pl.pallas_call(finish, out_shape=(shape((ROWS, D), BF), rows, rows, rows,...  4.42 us

profile of v3, /device:TPU:1, one launch (start us, length us, event | category | flops | bytes accessed | tf_op | source)
XLA Modules:
  0.0 143.2 jit_solution(5738805415561926119)
XLA Ops:
  1.3 0.0 copy-start
  1.3 0.7 copy-done
  2.0 0.1 broadcast_in_dim.35
  2.1 0.1 broadcast_in_dim.39
  2.1 0.0 copy-start.1
  2.1 0.1 broadcast_in_dim.37
  2.2 0.6 copy-done.1
  2.8 1.0 fusion
  3.8 135.0 %shard_map.137 = (bf16[128,3072]{1,0:T(8,128)(2,1)}, bf16[128,2048]{1,0:T(8,128)(2,1)}, bf16[128,2048]{1,0:T(8,128)(2,1)}, bf16[16,128,128]{2,1,0:T(8,128)(2,1)}, bf16[8,192,128]{2,1,0:T(8,128)(2,1)}) custom-call(bf16[128,2048]{1,0:T(8,128)(2,1)} %bitcast.21, bf16[128,2048]{1,0:T(8,128)(2,1)} %bitcast.22, bf16[128,2048]{1,0:T(8,128)(2,1)} %bitcast.23, ...), custom_call_target="tpu_custom_call" | custom-call | tf_op jit(solution)/shard_map/pallas_call | solution.py:561
  138.8 4.4 %shard_map.138 = (bf16[128,3072]{1,0:T(8,128)(2,1)}, bf16[128,2048]{1,0:T(8,128)(2,1)}, bf16[128,2048]{1,0:T(8,128)(2,1)}, bf16[128,2048]{1,0:T(8,128)(2,1)}, f32[192,128]{1,0:T(8,128)}) custom-call(bf16[128,3072]{1,0:T(8,128)(2,1)} %get-tuple-element.15.mixed_ref, bf16[128,2048]{1,0:T(8,128)(2,1)} %get-tuple-element.16.gk_ref, ...), custom_call_target="tpu_custom_call" | custom-call | tf_op jit(solution)/shard_map/pallas_call | solution.py:592
  (3 shorter events, 0.0 us)
Async XLA Ops:
  1.3 0.7 copy-start
  2.1 0.7 copy-start.1

commit v4 on v3

--- a/solution.py
+++ b/solution.py
@@ -70,27 +70,41 @@
     return pl.multiple_of(index, size)
 
 
-def finish(mixed_ref, gk_ref, gv_ref, gq_ref, zr_ref, cos_ref, sin_ref, perm_ref, mixed_out, gq_out, gk_out, gv_out, gw_out, wide, keys, values, sems):
-    ways = ((mixed_ref, wide, mixed_out), (gk_ref, keys, gk_out), (gv_ref, values, gv_out))
-    loads = [pltpu.make_async_copy(src, held, sems.at[i]) for i, (src, held, _) in enumerate(ways)]
-    stores = [pltpu.make_async_copy(held, dst, sems.at[3 + i]) for i, (_, held, dst) in enumerate(ways)]
+def finish(
+    mixed_hbm, gk_hbm, gv_hbm, raw_hbm, terms_hbm, cos_hbm, sin_hbm, perm_hbm,
+    mixed_out, gq_out, gk_out, gv_out, gw_out,
+    mixed, gk, gv, raw, terms, cos, sin, perm, gq, gw, load_sem, store_sem,
+):
+    pairs = (
+        (raw_hbm, raw), (cos_hbm, cos), (sin_hbm, sin), (perm_hbm, perm), (terms_hbm, terms),
+        (mixed_hbm, mixed), (gk_hbm, gk), (gv_hbm, gv),
+    )
+    loads = [pltpu.make_async_copy(src, dst, load_sem.at[i]) for i, (src, dst) in enumerate(pairs)]
+    pairs = ((gq, gq_out), (gw, gw_out), (mixed, mixed_out), (gk, gk_out), (gv, gv_out))
+    stores = [pltpu.make_async_copy(src, dst, store_sem.at[i]) for i, (src, dst) in enumerate(pairs)]
     for load in loads:
         load.start()
-    for load, store in zip(loads, stores):
+    for load in loads[:4]:
+        load.wait()
+    for h in range(HEADS):
+        part = raw[h]
+        turned = part.astype(F32) * cos[...] - nn(part, perm[...]) * sin[...]
+        gq[:, h * HD : (h + 1) * HD] = turned.astype(BF)
+    stores[0].start()
+    for load, store in zip(loads[5:], stores[2:]):
         load.wait()
         store.start()
-    for h in range(HEADS):
-        part = gq_ref[h]
-        turned = part.astype(F32) * cos_ref[...] - nn(part, perm_ref[...]) * sin_ref[...]
-        gq_out[:, h * HD : (h + 1) * HD] = turned.astype(BF)
-    gw_out[...] = sum(zr_ref[i].astype(F32) for i in range(8))
+    loads[4].wait()
+    gw[...] = sum(terms[i].astype(F32) for i in range(8))
+    stores[1].start()
     for store in stores:
         store.wait()
 
 
 def kernel(
-    q_hbm, k_hbm, v_hbm, cos_ref, sin_ref, perm_ref, w_hbm, cot_hbm, bucket_ref, cost_ref,
-    mixed_hbm, gk_hbm, gv_hbm, gq_hbm, zr_hbm,
+    q_hbm, k_hbm, v_hbm, pos_ref, freq_ref, perm_ref, w_hbm, cot_hbm, bucket_ref, cost_ref,
+    mixed_hbm, gk_hbm, gv_hbm, gq_hbm, zr_hbm, cos_hbm, sin_hbm,
+    cos_ref, sin_ref,
     q_ref, k_ref, v_ref, cot_ref, mixed_out, gk_out, gv_out,
     rin, rel, qh, kh, vh, kt, vt, wbuf, probs, ot, rl, att, dealt, att_tok,
     gd, gdh, dot_t, dq_t, gsend, grecv, cot_t, ct, at_all, gw_send, xr, zs, zr,
@@ -123,6 +137,8 @@
     for load in loads:
         load.start()
 
+    vt[HD:, :] = jnp.ones((16, TOKENS), BF)
+
     barrier = pltpu.get_barrier_semaphore()
 
     def greet(to):
@@ -163,6 +179,60 @@
     lanes = lambda h: pl.ds(al(h * HD, HD), HD)
     sibling = device(x, y, z, 1 - c)
     me8 = y * 2 + c
+
+    def hand_over_cotangent():
+        for j in range(1, 4):
+            view = ct.at[:, lanes((y + 4 - j) % 4 * 2 + c)]
+            wait(view, rsem.at[36 + j])
+            send(view, view, 19, 10, sibling)
+
+    angles = sum(
+        jnp.broadcast_to(pos_ref[a].astype(F32), (ROWS, ROWS)).T * freq_ref[a : a + 1] for a in range(3)
+    )
+    cos_ref[...] = jnp.cos(angles)
+    sin_ref[...] = jnp.sin(angles)
+
+    cos, sin, perm = cos_ref[...], sin_ref[...], perm_ref[...]
+
+    def turn(block, direction):
+        return block.astype(F32) * cos + direction * nn(block, perm) * sin
+
+    mine = pl.ds(al(sp * ROWS, ROWS), ROWS)
+
+    partner = (dp, z * 2 + 1 - xh)
+    theirs = pl.ds(al(partner[1] * ROWS, ROWS), ROWS)
+
+    def fill(n, src, side):
+        @pl.loop(0, 8)
+        def _(i):
+            part = src[:, lanes(i * 2 + side)]
+            rin[n, side, i] = part.T if n == 2 else turn(part, 1.0).astype(BF)
+
+    def cross(n):
+        send(rin.at[n, 1 - xh], rel.at[n], 21 + n, 44 + n, partner)
+
+    def along(n, view, dst, rows, s):
+        spot = dst.at[pl.ds(0, HD), rows] if n == 2 else dst.at[rows]
+        keep(view.at[z], spot, n)
+
+        @pl.loop(1, 8)
+        def _(j):
+            tz = lax.rem(z + j, 8)
+            send(view.at[tz], spot, s, n, (dp, tz * 2 + xh))
+
+    arrays = ((0, q_ref, qh), (1, k_ref, kh), (2, v_ref, vt))
+
+    def hand_on(n, dst):
+        wait(rel.at[n], rsem.at[44 + n])
+        along(n, rel.at[n], dst, theirs, 24 + n)
+
+    for n, src, _ in arrays[:2]:
+        loads[1 + n].wait()
+        fill(n, src, 1 - xh)
+        cross(n)
+    fill(0, q_ref, xh)
+    along(0, rin.at[0, xh], qh, mine, 0)
+
     loads[0].wait()
     for i in range(D // 128):
         cot_t[i * 128 : (i + 1) * 128, :] = cot_ref[:, i * 128 : (i + 1) * 128].T
@@ -173,51 +243,6 @@
         ty = (y + j) % 4
         send(cot_t.at[pl.ds(al(ty * 768, 768), 768)], ct.at[:, lanes(me8)], 10, 36 + j, device(x, ty, z, c))
 
-    def hand_over_cotangent():
-        for j in range(1, 4):
-            view = ct.at[:, lanes((y + 4 - j) % 4 * 2 + c)]
-            wait(view, rsem.at[36 + j])
-            send(view, view, 19, 10, sibling)
-
-    cos, sin, perm = cos_ref[...], sin_ref[...], perm_ref[...]
-
-    def turn(block, direction):
-        return block.astype(F32) * cos + direction * nn(block, perm) * sin
-
-    mine = pl.ds(al(sp * ROWS, ROWS), ROWS)
-
-    partner = (dp, z * 2 + 1 - xh)
-    theirs = pl.ds(al(partner[1] * ROWS, ROWS), ROWS)
-
-    def fill(n, src, side):
-        @pl.loop(0, 8)
-        def _(i):
-            part = src[:, lanes(i * 2 + side)]
-            rin[n, side, i] = part if n == 2 else turn(part, 1.0).astype(BF)
-
-    def cross(n):
-        send(rin.at[n, 1 - xh], rel.at[n], 21 + n, 44 + n, partner)
-
-    def along(n, view, dst, rows, s):
-        keep(view.at[z], dst.at[rows], n)
-
-        @pl.loop(1, 8)
-        def _(j):
-            tz = lax.rem(z + j, 8)
-            send(view.at[tz], dst.at[rows], s, n, (dp, tz * 2 + xh))
-
-    arrays = ((0, q_ref, qh), (1, k_ref, kh), (2, v_ref, vh))
-
-    def hand_on(n, dst):
-        wait(rel.at[n], rsem.at[44 + n])
-        along(n, rel.at[n], dst, theirs, 24 + n)
-
-    for n, src, _ in arrays[:2]:
-        loads[1 + n].wait()
-        fill(n, src, 1 - xh)
-        cross(n)
-    fill(0, q_ref, xh)
-    along(0, rin.at[0, xh], qh, mine, 0)
     fill(1, k_ref, xh)
     loads[3].wait()
     fill(2, v_ref, xh)
@@ -290,13 +315,13 @@
     along(1, rin.at[1, xh], kh, mine, 1)
     for n, _, dst in arrays[:2]:
         hand_on(n, dst)
-    along(2, rin.at[2, xh], vh, mine, 2)
+    along(2, rin.at[2, xh], vt, mine, 2)
     per_core(first_ring)
     cross(2)
     hand_over_cotangent()
     pass_on(0)
     per_core(first_ring_end)
-    hand_on(2, vh)
+    hand_on(2, vt)
     pass_on(1)
 
     wait(qh, rsem.at[0])
@@ -320,9 +345,7 @@
     pl.loop(4, TOKENS // QB)(weigh)
     pass_on(3)
 
-    wait(vh, rsem.at[2])
-    vt[:HD, :] = vh[...].T
-    vt[HD:, :] = jnp.ones((16, TOKENS), BF)
+    wait(vt.at[pl.ds(0, HD)], rsem.at[2])
 
     @pl.loop(0, TOKENS // QB)
     def _(b):
@@ -365,19 +388,19 @@
 
     def grad_of(h):
         total = sum(
-            nt(cot_ref[:, t * WIDE : (t + 1) * WIDE], wbuf[t, h % 2, h // 2].reshape(HD, WIDE))
+            nt(wbuf[t, h % 2, h // 2].reshape(HD, WIDE), cot_ref[:, t * WIDE : (t + 1) * WIDE])
             for t in range(PARTS)
         )
         gd[h] = total.astype(BF)
 
     grad_of(sp)
-    keep(gd.at[sp], gdh.at[mine], 4)
-
-    @pl.loop(1, 16)
+    keep(gd.at[sp], gdh.at[:, mine], 4)
+
+    @pl.loop(0, 15)
     def _(j):
-        h = lax.rem(sp + j, 16)
+        h = lax.rem(sp + 1 + lax.rem(j + 7, 15), 16)
         grad_of(h)
-        send(gd.at[h], gdh.at[mine], 4, 4, (dp, h))
+        send(gd.at[h], gdh.at[:, mine], 4, 4, (dp, h))
 
     wait(att_tok, rsem.at[3])
     def rows_of(ty, tc, first=0, count=ROWS):
@@ -402,10 +425,15 @@
     stores = [
         pltpu.make_async_copy(src, dst, lsem.at[4 + i])
         for i, (src, dst) in enumerate(
-            ((mixed_out, mixed_hbm), (gv_out, gv_hbm), (gk_out, gk_hbm), (grecv.at[2], gq_hbm), (zr, zr_hbm))
+            (
+                (mixed_out, mixed_hbm), (gv_out, gv_hbm), (gk_out, gk_hbm), (grecv.at[2], gq_hbm), (zr, zr_hbm),
+                (cos_ref, cos_hbm), (sin_ref, sin_hbm),
+            )
+
         )
     ]
-    stores[0].start()
+    for store in (stores[0], stores[5], stores[6]):
+        store.start()
 
     for m, step in ((0, 3), (1, 1)):
         ty = (y + step) % 4
@@ -415,13 +443,14 @@
             send(part, part, 18, 11, device(x, (y + 4 - step) % 4, z, c))
 
     kt[...] = kh[...].T
+    vh[...] = vt[:HD, :].T
 
     wait(gdh, rsem.at[4])
-    slots = [gdh[k * SLOT : (k + 1) * SLOT, :].astype(F32) for k in range(CLIPS)]
+    slots = [gdh[:, k * SLOT : (k + 1) * SLOT].astype(F32) for k in range(CLIPS)]
     for k in range(CLIPS):
         picked = sum(slots[r] * choose[r][k] for r in range(CLIPS))
         part = slice(k * SLOT, (k + 1) * SLOT)
-        dot_t[:, part] = (picked.T * rl[:, part]).astype(BF)
+        dot_t[:, part] = (picked * rl[:, part]).astype(BF)
 
     def give(n, t):
         @pl.when(t == sp)
@@ -436,7 +465,7 @@
 
     @pl.loop(0, TOKENS // QB)
     def _(i):
-        b = (i + sp // 2) % (TOKENS // QB)
+        b = (i + sp // 2 + 4) % (TOKENS // QB)
         rows = pl.ds(al(b * QB, QB), QB)
         low = probs[rows, :]
         value_grad = nt(low, dot_t[...]).astype(BF)
@@ -544,10 +573,8 @@
 
 def local(query, key_in, value, bucket, clip_cost, positions, out_weight, cotangent):
     _, _, axis_of, frequency = rotary_layout(HD)
-    angles = jnp.transpose(positions[:, 0, :].astype(F32))
-    angles = jnp.concatenate(
-        [jnp.broadcast_to(angles[:, a : a + 1], (ROWS, int(np.sum(axis_of == a)))) for a in range(3)], axis=1
-    ) * jnp.asarray(frequency, F32)
+    rates = np.zeros((8, HD), np.float32)
+    rates[axis_of, np.arange(HD)] = frequency
     perm = jnp.asarray(partner_matrix(), BF)
 
     vmem = pl.BlockSpec(memory_space=pltpu.VMEM)
@@ -556,14 +583,15 @@
     f32 = lambda *shape: pltpu.VMEM(shape, F32)
     shape = jax.ShapeDtypeStruct
     hbm = pl.BlockSpec(memory_space=pl.ANY)
-    cos, sin = jnp.cos(angles), jnp.sin(angles)
+    table = shape((ROWS, HD), F32)
     rows = shape((ROWS, TOKENS), BF)
-    mixed, grad_key, grad_value, raw_query, terms = pl.pallas_call(
+    mixed, grad_key, grad_value, raw_query, terms, cos, sin = pl.pallas_call(
         kernel,
-        out_shape=(shape((ROWS, D), BF), rows, rows, shape((16, ROWS, HD), BF), shape((8, 192, HD), BF)),
+        out_shape=(shape((ROWS, D), BF), rows, rows, shape((16, ROWS, HD), BF), shape((8, 192, HD), BF), table, table),
         in_specs=[hbm] * 3 + [vmem] * 3 + [hbm] * 2 + [smem] * 2,
-        out_specs=(hbm,) * 5,
+        out_specs=(hbm,) * 7,
         scratch_shapes=[
+            f32(ROWS, HD), f32(ROWS, HD),
             bf(ROWS, TOKENS), bf(ROWS, TOKENS), bf(ROWS, TOKENS), bf(ROWS, D),
             bf(ROWS, D), bf(ROWS, TOKENS), bf(ROWS, TOKENS),
             bf(3, 2, 8, ROWS, HD), bf(3, 8, ROWS, HD),
@@ -574,27 +602,31 @@
             f32(HD, TOKENS), f32(1, TOKENS),
             bf(TOKENS, HD), bf(TOKENS, HD),
             bf(2, ROWS, 1024),
-            bf(16, ROWS, HD), bf(TOKENS, HD),
+            bf(16, HD, ROWS), bf(HD, TOKENS),
             bf(HD, TOKENS), f32(HD, TOKENS),
             bf(3, 16, ROWS, HD), bf(3, 16, ROWS, HD),
             bf(D, ROWS), bf(768, 1024), bf(1024, 1024),
             bf(4, 192, 1024), bf(4, 192, 1024),
             bf(8, 192, HD), bf(8, 192, HD),
-            pltpu.SemaphoreType.DMA((27,)), pltpu.SemaphoreType.DMA((47,)), pltpu.SemaphoreType.DMA((9,)),
+            pltpu.SemaphoreType.DMA((27,)), pltpu.SemaphoreType.DMA((47,)), pltpu.SemaphoreType.DMA((11,)),
         ],
         compiler_params=pltpu.CompilerParams(
             collective_id=0, has_side_effects=True, vmem_limit_bytes=62 * 2**20
         ),
     )(
-        query[0], key_in[0], value[0], cos, sin, perm,
+        query[0], key_in[0], value[0], positions, jnp.asarray(rates), perm,
         out_weight, cotangent[0], bucket, clip_cost,
     )
     mixed, grad_query, grad_key, grad_value, grad_weight = pl.pallas_call(
         finish,
         out_shape=(shape((ROWS, D), BF), rows, rows, rows, shape((192, HD), F32)),
-        in_specs=[hbm] * 3 + [vmem] * 5,
-        out_specs=(hbm, vmem, hbm, hbm, vmem),
-        scratch_shapes=[bf(ROWS, D), bf(ROWS, TOKENS), bf(ROWS, TOKENS), pltpu.SemaphoreType.DMA((6,))],
+        in_specs=[hbm] * 8,
+        out_specs=(hbm,) * 5,
+        scratch_shapes=[
+            bf(ROWS, D), bf(ROWS, TOKENS), bf(ROWS, TOKENS), bf(16, ROWS, HD), bf(8, 192, HD),
+            f32(ROWS, HD), f32(ROWS, HD), bf(HD, HD), bf(ROWS, TOKENS), f32(192, HD),
+            pltpu.SemaphoreType.DMA((8,)), pltpu.SemaphoreType.DMA((5,)),
+        ],
     )(mixed, grad_key, grad_value, raw_query, terms, cos, sin, perm)
     return mixed[None], grad_query[None], grad_key[None], grad_value[None], grad_weight.T
 

time: 144 us -> 141 us (0.979)
  local copies, waits for them, and re-layouts: 1.5 us -> 0 us
    pallas_call x1, Pallas kernels: 135 us -> 137 us  [local(): pl.pallas_call(kernel, out_shape=(shape((ROWS, D), BF), rows, rows, shape...]
    pallas_call x1, Pallas kernels: 4.42 us -> 2.91 us  [local(): pl.pallas_call(finish, out_shape=(shape((ROWS, D), BF), rows, rows, rows,...]
where the time goes in v4:
time: 141 us
  Pallas kernels  140 us (99%)
    pallas_call x1, Pallas kernels, local(): pl.pallas_call(kernel, out_shape=(shape((ROWS, D), BF), rows, rows, shape...  137 us
    pallas_call x1, Pallas kernels, local(): pl.pallas_call(finish, out_shape=(shape((ROWS, D), BF), rows, rows, rows,...  2.91 us

profile of v4, /device:TPU:1, one launch (start us, length us, event | category | flops | bytes accessed | tf_op | source)
XLA Modules:
  0.0 141.1 jit_solution(5658855670450644915)
XLA Ops:
  1.3 136.9 %shard_map.137 = (bf16[128,3072]{1,0:T(8,128)(2,1)}, bf16[128,2048]{1,0:T(8,128)(2,1)}, bf16[128,2048]{1,0:T(8,128)(2,1)}, bf16[16,128,128]{2,1,0:T(8,128)(2,1)}...) custom-call(bf16[128,2048]{1,0:T(8,128)(2,1)} %bitcast.10, bf16[128,2048]{1,0:T(8,128)(2,1)} %bitcast.11, ...), custom_call_target="tpu_custom_call" | custom-call | tf_op jit(solution)/shard_map/pallas_call | solution.py:588
  138.2 2.9 %shard_map.138 = (bf16[128,3072]{1,0:T(8,128)(2,1)}, bf16[128,2048]{1,0:T(8,128)(2,1)}, bf16[128,2048]{1,0:T(8,128)(2,1)}, bf16[128,2048]{1,0:T(8,128)(2,1)}, f32[192,128]{1,0:T(8,128)}) custom-call(bf16[128,3072]{1,0:T(8,128)(2,1)} %get-tuple-element.17.mixed_hbm, bf16[128,2048]{1,0:T(8,128)(2,1)} %get-tuple-element.18.gk_hbm, ...), custom_call_target="tpu_custom_call" | custom-call | tf_op jit(solution)/shard_map/pallas_call | solution.py:620

commit v5 on v4

--- a/solution.py
+++ b/solution.py
@@ -211,27 +211,27 @@
     def cross(n):
         send(rin.at[n, 1 - xh], rel.at[n], 21 + n, 44 + n, partner)
 
-    def along(n, view, dst, rows, s):
+    def along(n, view, dst, rows, s, r):
         spot = dst.at[pl.ds(0, HD), rows] if n == 2 else dst.at[rows]
-        keep(view.at[z], spot, n)
+        keep(view.at[z], spot, r)
 
         @pl.loop(1, 8)
         def _(j):
             tz = lax.rem(z + j, 8)
-            send(view.at[tz], spot, s, n, (dp, tz * 2 + xh))
+            send(view.at[tz], spot, s, r, (dp, tz * 2 + xh))
 
     arrays = ((0, q_ref, qh), (1, k_ref, kh), (2, v_ref, vt))
 
     def hand_on(n, dst):
         wait(rel.at[n], rsem.at[44 + n])
-        along(n, rel.at[n], dst, theirs, 24 + n)
+        along(n, rel.at[n], dst, theirs, 24 + n, 47 if n == 2 else n)
 
     for n, src, _ in arrays[:2]:
         loads[1 + n].wait()
         fill(n, src, 1 - xh)
         cross(n)
     fill(0, q_ref, xh)
-    along(0, rin.at[0, xh], qh, mine, 0)
+    along(0, rin.at[0, xh], qh, mine, 0, 0)
 
     loads[0].wait()
     for i in range(D // 128):
@@ -312,10 +312,10 @@
         wait(wbuf.at[rest], rsem.at[13])
 
     per_core(first_ring_start)
-    along(1, rin.at[1, xh], kh, mine, 1)
+    along(1, rin.at[1, xh], kh, mine, 1, 1)
     for n, _, dst in arrays[:2]:
         hand_on(n, dst)
-    along(2, rin.at[2, xh], vt, mine, 2)
+    along(2, rin.at[2, xh], vt, mine, 2, 2)
     per_core(first_ring)
     cross(2)
     hand_over_cotangent()
@@ -343,17 +343,33 @@
     pl.loop(0, 4)(weigh)
     pass_on(2)
     pl.loop(4, TOKENS // QB)(weigh)
-    pass_on(3)
-
-    wait(vt.at[pl.ds(0, HD)], rsem.at[2])
+
+    def weighted(side, cols):
+        spans = [lanes(i * 2 + side) for i in range(8)]
+        left = jnp.concatenate([vt[:, span] for span in spans], axis=1)
+        right = jnp.concatenate([probs[span, cols] for span in spans], axis=0)
+        return nn(left, right)
+
+    wait(vt.at[pl.ds(0, HD), pl.ds(0, 8 * HD)], rsem.at[2])
 
     @pl.loop(0, TOKENS // QB)
     def _(b):
         cols = pl.ds(al(b * QB, QB), QB)
-        out = nn(vt[...], probs[:, cols])
-        scale = 1.0 / out[HD : HD + 1]
+        out = weighted(xh, cols)
+        rl[:, cols] = out[HD : HD + 1]
+        ot[:, cols] = out[:HD]
+
+    pass_on(3)
+
+    wait(vt.at[pl.ds(0, HD), pl.ds(0, 8 * HD)], rsem.at[47])
+
+    @pl.loop(0, TOKENS // QB)
+    def _(b):
+        cols = pl.ds(al(b * QB, QB), QB)
+        out = weighted(1 - xh, cols)
+        scale = 1.0 / (rl[:, cols] + out[HD : HD + 1])
         rl[:, cols] = scale
-        out = out[:HD] * scale
+        out = (ot[:, cols] + out[:HD]) * scale
         ot[:, cols] = out
         att[cols, :] = out.T.astype(BF)
 
@@ -608,7 +624,7 @@
             bf(D, ROWS), bf(768, 1024), bf(1024, 1024),
             bf(4, 192, 1024), bf(4, 192, 1024),
             bf(8, 192, HD), bf(8, 192, HD),
-            pltpu.SemaphoreType.DMA((27,)), pltpu.SemaphoreType.DMA((47,)), pltpu.SemaphoreType.DMA((11,)),
+            pltpu.SemaphoreType.DMA((27,)), pltpu.SemaphoreType.DMA((48,)), pltpu.SemaphoreType.DMA((11,)),
         ],
         compiler_params=pltpu.CompilerParams(
             collective_id=0, has_side_effects=True, vmem_limit_bytes=62 * 2**20

time: 141 us -> 141 us (level)
  no operation moved by 1% of the time
where the time goes in v5:
time: 141 us
  Pallas kernels  140 us (99%)
    pallas_call x1, Pallas kernels, local(): pl.pallas_call(kernel, out_shape=(shape((ROWS, D), BF), rows, rows, shape...  137 us
    pallas_call x1, Pallas kernels, local(): pl.pallas_call(finish, out_shape=(shape((ROWS, D), BF), rows, rows, rows,...  2.91 us

profile of v5, /device:TPU:1, one launch (start us, length us, event | category | flops | bytes accessed | tf_op | source)
XLA Modules:
  0.0 141.2 jit_solution(18286490885753114394)
XLA Ops:
  1.3 137.0 %shard_map.137 = (bf16[128,3072]{1,0:T(8,128)(2,1)}, bf16[128,2048]{1,0:T(8,128)(2,1)}, bf16[128,2048]{1,0:T(8,128)(2,1)}, bf16[16,128,128]{2,1,0:T(8,128)(2,1)}...) custom-call(bf16[128,2048]{1,0:T(8,128)(2,1)} %bitcast.10, bf16[128,2048]{1,0:T(8,128)(2,1)} %bitcast.11, ...), custom_call_target="tpu_custom_call" | custom-call | tf_op jit(solution)/shard_map/pallas_call | solution.py:604
  138.3 2.9 %shard_map.138 = (bf16[128,3072]{1,0:T(8,128)(2,1)}, bf16[128,2048]{1,0:T(8,128)(2,1)}, bf16[128,2048]{1,0:T(8,128)(2,1)}, bf16[128,2048]{1,0:T(8,128)(2,1)}, f32[192,128]{1,0:T(8,128)}) custom-call(bf16[128,3072]{1,0:T(8,128)(2,1)} %get-tuple-element.17.mixed_hbm, bf16[128,2048]{1,0:T(8,128)(2,1)} %get-tuple-element.18.gk_hbm, ...), custom_call_target="tpu_custom_call" | custom-call | tf_op jit(solution)/shard_map/pallas_call | solution.py:636
